TPU v7x, 256 devices: a whole 4x4x8 slice. The times are simulated.
256 devices in a mesh: ctx: 32 (over y, x, z_hi), fsdp: 8 (over z_lo, core).
Axes of the slice: x: 4, y: 4, z: 8 (z_hi: 2, z_lo: 4; z = z_hi * 4 + z_lo), core: 2. Of those that a mesh axis runs over, the one named last changes fastest.
Arguments:
- proj: bfloat16 [8, 4096, 12288], P('fsdp', 'ctx'), may hold values from -6 to 6
- short_taps: float32 [7, 12288], P(None, 'fsdp'), may hold values from -2 to 2
- long_filter: float32 [128, 256], P(None, 'fsdp'), may hold values from -0.5 to 0.5
- skip: float32 [4096], P('fsdp'), may hold values from -3 to 3
- grad_out: bfloat16 [8, 4096, 4096], P('fsdp', 'ctx'), may hold values from -6 to 6
- starts: int32 [8, 32, 4], P('fsdp', 'ctx'), may hold values from 0 to 128, as said below
Outputs:
- mixed_out: bfloat16 [8, 4096, 4096], P('fsdp', 'ctx')
- grad_proj: bfloat16 [8, 4096, 12288], P('fsdp', 'ctx')
- grad_short: float32 [7, 12288], P(None, 'fsdp')
- grad_long: float32 [128, 256], P(None, 'fsdp')
- grad_skip: float32 [4096], P('fsdp')
Inputs may be any that keep to these rules, and one draw needn't show every extreme that they name: Each list holds positions, within one device's 128 positions, at which documents start, increasing and without repeats; entries equal to 128 are empty and come after all others. Every window's first position starts a document.
All inputs are finite; a program needn't handle non-finite values.
Results may differ from a plain program's by a relative error of at most 0.007.
Values may be sent and summed in bfloat16 or wider, within the bound.
No kernel may reach another device: no remote copies, remote signals or barrier semaphores. Data moves between devices by JAX's collectives and lax.ppermute only.
A program may use at most 128 MiB of HBM per device.

v0:
```python
import jax
import jax.numpy as jnp
from jax import lax
from jax.sharding import PartitionSpec as P

C = 4096
GROUP = 16
LEN = 128
SHORT = 7


far_back = 1 << 29


def prefix(value, axis, join, neutral):
    count, mine = (lax.axis_size(axis), lax.axis_index(axis))
    pieces = lax.all_gather(value, axis)
    so_far = jnp.full_like(value, 0) + jnp.asarray(neutral, value.dtype)

    def step(position, so_far):
        longer = join(so_far, pieces[position])
        return jnp.where(position < mine, longer, so_far)

    return lax.fori_loop(0, count - 1, step, so_far)


def passed_along(block, axis, distance):
    devices = range(lax.axis_size(axis))
    route = [(i - distance, i) for i in devices if i - distance in devices]
    return lax.ppermute(block, axis, route)


def toeplitz_tiles(values, rows_count, cols_count, low_diff):
    groups, taps_count = values.shape
    period = rows_count + cols_count + taps_count
    period_row = jnp.concatenate(
        [values, jnp.zeros((groups, period - taps_count), values.dtype)], axis=1
    )
    period_row = jnp.roll(period_row, low_diff, axis=1)
    repeated = jnp.tile(period_row, (1, rows_count))[:, : rows_count * (period - 1)]
    return repeated.reshape(groups, rows_count, period - 1)[:, :, :cols_count]


def lag_totals(product, rows_count, cols_count):
    groups = product.shape[0]
    flattened = product.reshape(groups, rows_count * cols_count)
    flattened = jnp.pad(flattened, ((0, 0), (0, rows_count)))
    totals = jnp.sum(flattened.reshape(groups, rows_count, cols_count + 1), axis=1)
    return totals[:, LEN:0:-1]


def body(proj, short_taps, long_filter, skip, grad_out, starts):
    taps_all, filt_all, skip_all = (
        lax.all_gather(short_taps, "fsdp", axis=1, tiled=True),
        lax.all_gather(long_filter, "fsdp", axis=1, tiled=True),
        lax.all_gather(skip, "fsdp", axis=0, tiled=True),
    )
    source = proj[0]
    tok_rows = source.shape[0]
    win_rows = tok_rows + LEN
    groups = C // GROUP
    block_groups = min(groups, 32)
    block_count = groups // block_groups
    positions = jnp.arange(tok_rows, dtype=jnp.int32)
    listed = starts[0, 0]
    usable = listed < tok_rows
    own_last = jnp.max(jnp.where(usable, listed, -far_back)).reshape(1)
    ctx_index = lax.axis_index("ctx")
    placed = jnp.where(own_last >= 0, own_last + ctx_index * tok_rows, -far_back)
    before = prefix(placed, "ctx", jnp.maximum, jnp.full((1,), -far_back, jnp.int32))
    prior_start = before[0] - ctx_index * tok_rows
    candidates = jnp.where(
        usable[None, :] & (listed[None, :] <= positions[:, None]), listed[None, :], -far_back
    )
    last_local = jnp.maximum(prior_start, jnp.max(candidates, axis=1))
    short_tail = passed_along(source[tok_rows - (SHORT - 1) :], "ctx", 1)
    padded = jnp.concatenate([short_tail, source], axis=0)
    linked_rows = [(last_local <= positions - offset)[:, None] for offset in range(SHORT)]
    earlier_rows = [
        padded[SHORT - 1 - offset : SHORT - 1 - offset + tok_rows] for offset in range(SHORT)
    ]
    featured = jnp.zeros((tok_rows, 3 * C), jnp.float32)
    for offset in range(SHORT):
        featured = featured + taps_all[offset] * jnp.where(
            linked_rows[offset], earlier_rows[offset].astype(jnp.float32), 0.0
        )
    query_feat = featured[:, :C]
    key_feat = featured[:, C : 2 * C]
    value_feat = featured[:, 2 * C :]
    gating = (key_feat * value_feat).astype(jnp.bfloat16)
    gate_tail = passed_along(gating[tok_rows - (LEN - 1) :], "ctx", 1)
    window = jnp.concatenate([jnp.zeros((1, C), jnp.bfloat16), gate_tail, gating], axis=0)
    window_cols = window.T.reshape(groups, GROUP, win_rows)
    window_mask = last_local[:, None] <= (jnp.arange(win_rows, dtype=jnp.int32) - LEN)[None, :]
    reversed_taps = filt_all[::-1].astype(jnp.bfloat16).T
    zero_half = jnp.zeros((), jnp.bfloat16)
    upstream = grad_out[0].astype(jnp.float32)
    through = upstream * query_feat
    grad_long_in = through.astype(jnp.bfloat16)
    grad_cols = grad_long_in.T.reshape(groups, GROUP, tok_rows)

    def group_block(matrix, block_id):
        return lax.dynamic_slice_in_dim(matrix, block_id * block_groups, block_groups, 0)

    def ahead_tiles(block_id):
        return jnp.where(
            window_mask[None],
            toeplitz_tiles(group_block(reversed_taps, block_id), tok_rows, win_rows, 1),
            zero_half,
        )

    def filter_block(rows_blk, win_blk):
        product = jnp.einsum("gct,gcs->gts", rows_blk, win_blk, preferred_element_type=jnp.float32)
        return lag_totals(jnp.where(window_mask[None], product, 0.0), tok_rows, win_rows)

    def joint_block(block_id, state):
        long_cols, spread_cols, lag_grid = state
        tiles = ahead_tiles(block_id)
        win_blk = group_block(window_cols, block_id)
        rows_blk = group_block(grad_cols, block_id)
        fwd_out = jnp.einsum("gcs,gts->gct", win_blk, tiles, preferred_element_type=jnp.float32)
        bwd_out = jnp.einsum("gct,gts->gcs", rows_blk, tiles, preferred_element_type=jnp.float32)
        start_row = block_id * block_groups
        long_cols = lax.dynamic_update_slice_in_dim(long_cols, fwd_out, start_row, 0)
        spread_cols = lax.dynamic_update_slice_in_dim(spread_cols, bwd_out, start_row, 0)
        lag_grid = lax.dynamic_update_slice_in_dim(
            lag_grid, filter_block(rows_blk, win_blk), start_row, 0
        )
        return (long_cols, spread_cols, lag_grid)

    long_cols, spread_cols, lag_grid = lax.fori_loop(
        0,
        block_count,
        joint_block,
        (
            jnp.zeros((groups, GROUP, tok_rows), jnp.float32),
            jnp.zeros((groups, GROUP, win_rows), jnp.float32),
            jnp.zeros((groups, LEN), jnp.float32),
        ),
    )
    spread = spread_cols.reshape(C, win_rows).T
    returned = passed_along(spread[1:LEN], "ctx", -1)
    grad_gate = spread[LEN:] + jnp.concatenate(
        [jnp.zeros((tok_rows - (LEN - 1), C), jnp.float32), returned], axis=0
    )
    long_out = long_cols.reshape(C, tok_rows).T
    gate_f = gating.astype(jnp.float32)
    combined = long_out + skip_all * gate_f
    mixed_out = (query_feat * combined).astype(jnp.bfloat16)
    grad_query = upstream * combined
    grad_gate = grad_gate + skip_all * through
    grad_feat = jnp.concatenate([grad_query, grad_gate * value_feat, grad_gate * key_feat], axis=1)
    spread_short = jnp.zeros((tok_rows + SHORT - 1, 3 * C), jnp.float32)
    for offset in range(SHORT):
        contrib = taps_all[offset] * jnp.where(linked_rows[offset], grad_feat, 0.0)
        spread_short = spread_short + jnp.pad(contrib, ((SHORT - 1 - offset, offset), (0, 0)))
    returned_short = passed_along(spread_short[: SHORT - 1], "ctx", -1)
    grad_source = spread_short[SHORT - 1 :] + jnp.concatenate(
        [jnp.zeros((tok_rows - (SHORT - 1), 3 * C), jnp.float32), returned_short], axis=0
    )
    short_parts = []
    for offset in range(SHORT):
        earlier = jnp.where(linked_rows[offset], earlier_rows[offset].astype(jnp.float32), 0.0)
        short_parts.append(jnp.sum(grad_feat * earlier, axis=0))
    scaling = float(lax.axis_size("fsdp") * lax.axis_size("ctx") * tok_rows) ** (-0.5)
    grad_terms = (
        jnp.stack(short_parts) * scaling,
        lag_grid.T * scaling,
        jnp.sum(through * gate_f, axis=0) * scaling,
    )
    summed = lax.psum((grad_terms[0], grad_terms[1], grad_terms[2]), "ctx")
    reduced = (
        lax.psum_scatter(summed[0], "fsdp", scatter_dimension=1, tiled=True),
        lax.psum_scatter(summed[1], "fsdp", scatter_dimension=1, tiled=True),
        lax.psum_scatter(summed[2], "fsdp", scatter_dimension=0, tiled=True),
    )
    return (
        mixed_out[None],
        grad_source.astype(jnp.bfloat16)[None],
        reduced[0],
        reduced[1],
        reduced[2],
    )


def solution(mesh):
    placed = (
        P("fsdp", "ctx", None),
        P(None, "fsdp"),
        P(None, "fsdp"),
        P("fsdp"),
        P("fsdp", "ctx", None),
        P("fsdp", "ctx", None),
    )
    return jax.shard_map(
        body,
        mesh=mesh,
        in_specs=placed,
        out_specs=(
            P("fsdp", "ctx", None),
            P("fsdp", "ctx", None),
            P(None, "fsdp"),
            P(None, "fsdp"),
            P("fsdp"),
        ),
        check_vma=False,
    )
```

profile of v0, /device:TPU:32, one launch (start us, length us, event | category | flops | bytes accessed | tf_op | source)
XLA Modules:
  0.0 1028.5 jit_solution(2417254801992805471)
XLA Ops:
  8.9 8.9 collective-permute-start
  19.7 3.5 copy.27
  25.9 22.6 %all-reduce.12 = s32[32]{0:T(128)S(1)} all-reduce(s32[32]{0:T(128)S(1)} %dynamic-update-slice), channel_id=1, replica_groups=mesh['ctx'=32,'fsdp'=8] {'ctx'}, use_global_device_ids=true, to_apply=%add.12 | all-reduce | flops 32 | bytes 256
  48.4 38.9 %while.33 = (s32[]{:T(128)}, s32[1]{0:T(128)}, s32[]{:T(128)}, s32[32,1]{0,1:T(1,128)S(1)}, s32[]{:T(128)}) while((s32[]{:T(128)}, s32[1]{0:T(128)}, s32[]{:T(128)}, s32[32,1]{0,1:T(1,128)S(1)}, s32[]{:T(128)}) %tuple.109), condition=%wide.region_2.3_spmd, body=%wide.region_1.2_spmd.sunk | while | flops 5 | bytes 107 | solution.py:24
  87.4 13.5 %all_gather.15 = f32[7,12288]{1,0:T(8,128)S(1)} all-gather(f32[7,1536]{1,0:T(8,128)S(1)} %copy-done.20), channel_id=1, replica_groups=mesh['ctx'=32,'fsdp'=8] {'fsdp'}, dimensions={1}, use_global_device_ids=true | all-gather | bytes 387072 | tf_op jit(solution)/shard_map/all_gather | solution.py:54
  103.7 3.6 copy.28
  107.4 26.2 %multiply_add_fusion = f32[128,12288]{0,1:T(8,128)S(1)} fusion(bf16[128,12288]{0,1:T(8,128)(2,1)S(1)} %bitcast.87, f32[12288]{0:T(1024)S(1)} %bitcast.101, f32[12288]{0:T(1024)S(1)} %bitcast.103, f32[12288]{0:T(1024)S(1)} %bitcast.95, f32[12288]{0:T(1024)S(1)} %bitcast.105, f32[12288]{0:T(1024)S(1)} %bitcast.97, f32[12288]{0:T(1024)S(1)} %bitcast.107, ...), kind=kLoop, calls=%fused_computation.51 | loop fusion | flops 70778880 | bytes 9929600 | tf_op jit(solution)/shard_map/add | solution.py:84
  140.2 2.9 collective-permute-start.1
  143.1 54.7 %all_gather.18 = bf16[128,256]{0,1:T(8,128)(2,1)S(1)} all-gather(bf16[128,32]{0,1:T(8,128)(2,1)S(1)} %convert.13), channel_id=1, replica_groups=mesh['ctx'=32,'fsdp'=8] {'fsdp'}, dimensions={1}, use_global_device_ids=true | all-gather | bytes 73728 | tf_op jit(solution)/shard_map/all_gather | solution.py:55
  198.6 3.8 pad_maximum_fusion.2
  206.3 314.6 %while.34 = (s32[]{:T(128)}, f32[256,16,128]{2,1,0:T(8,128)}, f32[256,16,256]{2,1,0:T(8,128)}, f32[256,128]{1,0:T(8,128)S(1)}, bf16[256,16,256]{2,1,0:T(8,128)(2...) while((s32[]{:T(128)}, f32[256,16,128]{2,1,0:T(8,128)}, ...), condition=%wide.region_6.7_spmd.clone, body=%wide.region_4.6_spmd.clone.sunk | while | flops 104886240 | bytes 69137104 | solution.py:131
  212.4 9.6 reshape.152
  222.0 2.9 fusion.42
  231.4 8.0 reshape.153
  239.3 3.3 reduce_sum.106
  242.8 3.1 fusion.41
  251.7 9.6 reshape.152
  270.7 8.0 reshape.153
  278.6 3.3 reduce_sum.106
  282.1 3.1 fusion.41
  291.0 9.6 reshape.152
  300.7 2.9 fusion.42
  310.0 8.0 reshape.153
  317.9 3.3 reduce_sum.106
  321.4 3.1 fusion.41
  330.3 9.6 reshape.152
  349.2 8.0 reshape.153
  357.2 3.3 reduce_sum.106
  360.7 3.0 fusion.41
  369.5 9.6 reshape.152
  379.2 2.9 fusion.42
  388.5 8.0 reshape.153
  396.5 3.3 reduce_sum.106
  400.0 3.1 fusion.41
  408.8 9.6 reshape.152
  427.8 8.0 reshape.153
  435.8 3.3 reduce_sum.106
  439.3 3.0 fusion.41
  448.1 9.6 reshape.152
  467.1 8.0 reshape.153
  475.1 3.3 reduce_sum.106
  478.5 3.0 fusion.41
  487.4 9.6 reshape.152
  497.1 2.9 fusion.42
  506.4 8.0 reshape.153
  514.4 3.3 reduce_sum.106
  517.9 3.1 fusion.41
  520.9 3.6 slice.173
  527.7 13.0 %all-gather = f32[8,1,512]{2,1,0:T(1,128)S(1)} all-gather(f32[1,1,512]{2,1,0:T(1,128)} %bitcast.117), channel_id=1, replica_groups=mesh['ctx'=32,'fsdp'=8] {'fsdp'}, dimensions={0}, use_global_device_ids=true | all-gather | bytes 18432 | tf_op jit(solution)/shard_map/all_gather | solution.py:56
  540.7 25.5 %all-reduce.13 = f32[4096]{0:T(1024)S(1)} all-reduce(f32[4096]{0:T(1024)S(1)} %broadcast_multiply_fusion.1), channel_id=4, replica_groups=mesh['ctx'=32,'fsdp'=8] {'fsdp'}, use_global_device_ids=true, to_apply=%region_20.21.clone | all-reduce | flops 4096 | bytes 32768
  567.0 56.5 %collective-permute-done.2 = f32[127,4096]{0,1:T(8,128)} collective-permute-done((f32[127,4096]{0,1:T(8,128)}, f32[127,4096]{0,1:T(8,128)}, u32[]{:S(2)}, u32[]{:S(2)}) %collective-permute-start.2) | collective-permute-done | bytes 2080800 | tf_op jit(solution)/shard_map/ppermute | solution.py:30
  623.4 6.2 slice_multiply_fusion
  632.2 18.2 %multiply_reduce_fusion = (f32[12288]{0:T(1024)}, f32[12288]{0:T(1024)}, f32[12288]{0:T(1024)}, f32[128,12288]{0,1:T(8,128)}) fusion(pred[128]{0:T(512)(128)(4,1)S(1)} %copy-done.23, bf16[128,12288]{0,1:T(8,128)(2,1)S(1)} %bitcast.88, bf16[6,12288]{0,1:T(8,128)(2,1)S(1)} %copy-done.2, f32[128,4096]{0,1:T(8,128)S(1)} %slice_multiply_fusion.1, ...), kind=kLoop, calls=%fused_computation.37 | loop fusion | flops 39284736 | bytes 16073088 | tf_op jit(solution)/shard_map/reduce_sum | solution.py:164
  650.4 14.5 %multiply_reduce_fusion.1 = (f32[12288]{0:T(1024)S(1)}, f32[12288]{0:T(1024)}, f32[12288]{0:T(1024)}, f32[128,12288]{0,1:T(8,128)}) fusion(pred[128]{0:T(512)(128)(4,1)S(1)} %copy-done.25, bf16[128,12288]{0,1:T(8,128)(2,1)S(1)} %bitcast.89, bf16[6,12288]{0,1:T(8,128)(2,1)S(1)} %copy-done.2, f32[128,4096]{0,1:T(8,128)S(1)} %slice_multiply_fusion.1, ...), kind=kLoop, calls=%fused_computation.38 | loop fusion | flops 39284736 | bytes 16073088 | tf_op jit(solution)/shard_map/reduce_sum | solution.py:164
  664.9 10.6 %multiply_reduce_fusion.6 = (f32[12288]{0:T(1024)S(1)}, f32[128,12288]{0,1:T(8,128)}, f32[128,12288]{0,1:T(8,128)}, f32[128,12288]{0,1:T(8,128)}) fusion(pred[128]{0:T(512)(128)(4,1)S(1)} %copy-done.31, bf16[1,128,12288]{1,2,0:T(8,128)(2,1)S(1)} %copy.27, f32[128,4096]{0,1:T(8,128)S(1)} %slice_multiply_fusion.1, f32[128,4096]{0,1:T(8,128)S(1)} %get-tuple-element.371, ...), kind=kLoop, calls=%fused_computation.43 | loop fusion | flops 18862080 | bytes 28508544 | tf_op jit(solution)/shard_map/reduce_sum | solution.py:164
  675.5 13.9 %select_multiply_fusion.4 = (f32[128,12288]{0,1:T(8,128)}, f32[128,12288]{0,1:T(8,128)}) fusion(f32[12288]{0:T(1024)S(1)} %bitcast.98, pred[128]{0:T(512)(128)(4,1)S(1)} %get-tuple-element.398, f32[128,4096]{0,1:T(8,128)S(1)} %slice_multiply_fusion.1, f32[128,4096]{0,1:T(8,128)S(1)} %get-tuple-element.371, f32[128,4096]{0,1:T(8,128)S(1)} %get-tuple-element.385, ...), kind=kLoop, calls=%fused_computation.48 | loop fusion | flops 9437184 | bytes 18972928 | tf_op jit(solution)/shard_map/mul | solution.py:155
  689.5 24.6 %pad_add_fusion = f32[134,12288]{0,1:T(8,128)S(1)} fusion(f32[128,12288]{0,1:T(8,128)} %get-tuple-element.382, f32[128,12288]{0,1:T(8,128)} %get-tuple-element.381, f32[128,12288]{0,1:T(8,128)} %get-tuple-element.384, f32[128,12288]{0,1:T(8,128)} %get-tuple-element.377, f32[128,12288]{0,1:T(8,128)} %get-tuple-element.383, f32[128,12288]{0,1:T(8,128)S(1)} %copy-done.3, ...), kind=kLoop, calls=%fused_computation.23 | loop fusion | flops 9879552 | bytes 50626560 | tf_op jit(solution)/shard_map/add | solution.py:156
  714.1 4.5 copy-done.1
  721.4 4.5 copy.30
  730.0 45.2 %collective-permute-done.3 = f32[6,12288]{1,0:T(8,128)S(1)} collective-permute-done((f32[6,12288]{1,0:T(8,128)S(1)}, f32[6,12288]{1,0:T(8,128)S(1)}, u32[]{:S(2)}, u32[]{:S(2)}) %collective-permute-start.3) | collective-permute-done | bytes 294944 | tf_op jit(solution)/shard_map/ppermute | solution.py:30
  775.2 4.0 copy.31
  779.2 8.2 fusion.18
  790.1 8.1 reduce-scatter.3.cloned.1.call-done
  798.3 223.4 %all-reduce.14 = (f32[7,1536]{1,0:T(8,128)}, f32[128,32]{0,1:T(8,128)}, f32[512]{0:T(512)}) all-reduce(f32[7,1536]{1,0:T(8,128)} %reduce-scatter.3.cloned.1.call-done, f32[128,32]{0,1:T(8,128)} %reduce-scatter.5.cloned.1.call-done, f32[512]{0:T(512)S(1)} %dynamic-slice.2), channel_id=1, replica_groups=mesh['ctx'=32,'fsdp'=8] {'ctx'}, use_global_device_ids=true, to_apply=%region_14.15 | all-reduce | flops 15360 | bytes 122880 | tf_op jit(solution)/shard_map/psum | solution.py:171
  (245 shorter events, 163.7 us)
Async XLA Ops:
  7.2 17.3 %copy-start.33 = (u32[256]{0:T(256)S(1)}, u32[256]{0:T(256)}, u32[]{:S(2)}) copy-start(u32[256]{0:T(256)} %constant.169) | copy-start | bytes 3076
  7.2 96.3 %copy-start.32 = (s32[1,1,4]{2,1,0:T(1,128)S(1)}, s32[1,1,4]{2,1,0:T(1,128)}, u32[]{:S(2)}) copy-start(s32[1,1,4]{2,1,0:T(1,128)} %param.15) | copy-start | bytes 52
  7.2 80.2 %copy-start.20 = (f32[7,1536]{1,0:T(8,128)S(1)}, f32[7,1536]{1,0:T(8,128)}, u32[]{:S(2)}) copy-start(f32[7,1536]{1,0:T(8,128)} %param.11) | copy-start | bytes 129028
  7.2 782.9 %reduce-scatter.5.cloned.1.call-start = ((), (), s32[]{:S(2)}) async-start(), calls=%async_computation.3 | async-start | bytes 147456 | tf_op jit(solution)/shard_map/reduce_scatter | solution.py:174
  8.9 94.8 %collective-permute-start = (bf16[6,12288]{1,0:T(8,128)(2,1)}, bf16[6,12288]{1,0:T(8,128)(2,1)}, u32[]{:S(2)}, u32[]{:S(2)}) collective-permute-start(bf16[6,12288]{1,0:T(8,128)(2,1)} %slice_bitcast_fusion), channel_id=1, source_target_pairs={{0,8},{8,16},{16,24},{24,32},{32,40},{40,48},{48,56},{56,64},{64,7... | collective-permute-start | bytes 442376 | tf_op jit(solution)/shard_map/ppermute | solution.py:30
  101.2 32.4 %copy-start.7 = (f32[1,12288]{1,0:T(1,128)}, f32[1,12288]{1,0:T(1,128)S(1)}, u32[]{:S(2)}) copy-start(f32[1,12288]{1,0:T(1,128)S(1)} %get-tuple-element.387) | copy-start | bytes 147460
  101.2 32.4 %copy-start.9 = (f32[1,12288]{1,0:T(1,128)}, f32[1,12288]{1,0:T(1,128)S(1)}, u32[]{:S(2)}) copy-start(f32[1,12288]{1,0:T(1,128)S(1)} %get-tuple-element.388) | copy-start | bytes 147460
  101.2 32.4 %copy-start.11 = (f32[1,12288]{1,0:T(1,128)}, f32[1,12288]{1,0:T(1,128)S(1)}, u32[]{:S(2)}) copy-start(f32[1,12288]{1,0:T(1,128)S(1)} %get-tuple-element.390) | copy-start | bytes 147460
  101.2 32.4 %copy-start.13 = (f32[1,12288]{1,0:T(1,128)}, f32[1,12288]{1,0:T(1,128)S(1)}, u32[]{:S(2)}) copy-start(f32[1,12288]{1,0:T(1,128)S(1)} %get-tuple-element.392) | copy-start | bytes 147460
  103.6 30.0 %copy-start.30 = (pred[128]{0:T(512)(128)(4,1)}, pred[128]{0:T(512)(128)(4,1)S(1)}, u32[]{:S(2)}) copy-start(pred[128]{0:T(512)(128)(4,1)S(1)} %get-tuple-element.373) | copy-start | bytes 388
  103.7 3.7 copy-start.22
  103.7 3.7 copy-start.24
  103.7 3.7 copy-start.26
  103.7 3.7 copy-start.28
  107.3 29.0 %copy-start.5 = (bf16[1,128,4096]{1,2,0:T(8,128)(2,1)S(1)}, bf16[1,128,4096]{1,2,0:T(8,128)(2,1)}, u32[]{:S(2)}) copy-start(bf16[1,128,4096]{1,2,0:T(8,128)(2,1)} %copy.29) | copy-start | bytes 3145732
  133.6 2.7 copy-start
  136.3 6.8 copy-start.21
  137.8 1.0 copy-start.4
  140.2 58.4 %collective-permute-start.1 = (bf16[127,4096]{0,1:T(8,128)(2,1)}, bf16[127,4096]{0,1:T(8,128)(2,1)}, u32[]{:S(2)}, u32[]{:S(2)}) collective-permute-start(bf16[127,4096]{0,1:T(8,128)(2,1)} %slice.171), channel_id=1, source_target_pairs={{0,8},{8,16},{16,24},{24,32},{32,40},{40,48},{48,56},{56,64},{64,7... | collective-permute-start | bytes 3121160 | tf_op jit(solution)/shard_map/ppermute | solution.py:30
  524.5 99.0 %collective-permute-start.2 = (f32[127,4096]{0,1:T(8,128)}, f32[127,4096]{0,1:T(8,128)}, u32[]{:S(2)}, u32[]{:S(2)}) collective-permute-start(f32[127,4096]{0,1:T(8,128)} %slice.173), channel_id=1, source_target_pairs={{8,0},{16,8},{24,16},{32,24},{40,32},{48,40},{56,48},{64,56},{72,6... | collective-permute-start | bytes 6242312 | tf_op jit(solution)/shard_map/ppermute | solution.py:30
  566.9 231.3 %reduce-scatter.3.cloned.1.call-start = ((), (), s32[]{:S(2)}) async-start(), calls=%async_computation.2 | async-start | bytes 442368 | tf_op jit(solution)/shard_map/reduce_scatter | solution.py:173
  629.6 2.5 copy-start.2
  629.6 2.5 copy-start.14
  629.6 2.5 copy-start.23
  629.6 2.5 copy-start.29
  632.2 18.2 %copy-start.12 = (f32[1,12288]{1,0:T(1,128)S(1)}, f32[1,12288]{1,0:T(1,128)}, u32[]{:S(2)}) copy-start(f32[1,12288]{1,0:T(1,128)} %copy-done.11) | copy-start | bytes 147460
  632.2 18.2 %copy-start.25 = (pred[128]{0:T(512)(128)(4,1)S(1)}, pred[128]{0:T(512)(128)(4,1)}, u32[]{:S(2)}) copy-start(pred[128]{0:T(512)(128)(4,1)} %copy-done.24) | copy-start | bytes 388
  632.2 18.2 %copy-start.27 = (pred[128]{0:T(512)(128)(4,1)S(1)}, pred[128]{0:T(512)(128)(4,1)}, u32[]{:S(2)}) copy-start(pred[128]{0:T(512)(128)(4,1)} %copy-done.26) | copy-start | bytes 388
  650.4 14.5 %copy-start.8 = (f32[1,12288]{1,0:T(1,128)S(1)}, f32[1,12288]{1,0:T(1,128)}, u32[]{:S(2)}) copy-start(f32[1,12288]{1,0:T(1,128)} %copy-done.7) | copy-start | bytes 147460
  650.4 14.5 %copy-start.10 = (f32[1,12288]{1,0:T(1,128)S(1)}, f32[1,12288]{1,0:T(1,128)}, u32[]{:S(2)}) copy-start(f32[1,12288]{1,0:T(1,128)} %copy-done.9) | copy-start | bytes 147460
  650.4 14.5 %copy-start.31 = (pred[128]{0:T(512)(128)(4,1)S(1)}, pred[128]{0:T(512)(128)(4,1)}, u32[]{:S(2)}) copy-start(pred[128]{0:T(512)(128)(4,1)} %copy-done.30) | copy-start | bytes 388
  675.5 13.9 %copy-start.3 = (f32[128,12288]{0,1:T(8,128)S(1)}, f32[128,12288]{0,1:T(8,128)}, u32[]{:S(2)}) copy-start(f32[128,12288]{0,1:T(8,128)} %get-tuple-element.378) | copy-start | bytes 18874372
  714.1 4.5 copy-start.1
  721.4 5.9 copy-start.15
  721.4 5.9 copy-start.16
  721.4 5.9 copy-start.17
  721.4 5.9 copy-start.18
  721.4 5.9 copy-start.19
  721.4 7.3 copy-start.6
  726.0 49.2 %collective-permute-start.3 = (f32[6,12288]{1,0:T(8,128)S(1)}, f32[6,12288]{1,0:T(8,128)S(1)}, u32[]{:S(2)}, u32[]{:S(2)}) collective-permute-start(f32[6,12288]{1,0:T(8,128)S(1)} %copy.30), channel_id=1, source_target_pairs={{8,0},{16,8},{24,16},{32,24},{40,32},{48,40},{56,48},{64,56},{72,6... | collective-permute-start | bytes 884744 | tf_op jit(solution)/shard_map/ppermute | solution.py:30
Sparse Core Ops, SparseCore 0:
  567.1 120.0 reduce-scatter.4
  730.1 68.0 reduce-scatter.2
where the time goes:
time: 1030 us
  blocking collectives  353 us (34%)
  local copies, waits for them, and re-layouts  292 us (28%)
  other arithmetic  160 us (16%)
  waiting for transfers between devices  110 us (11%)
  matrix products  61.7 us (6%)
  loops' own time  21.4 us (2%)
  between operations  16.4 us (2%)
  starting transfers between devices  14.4 us (1%)
    psum x1, blocking collectives, body(): summed = lax.psum((grad_terms[0], grad_terms[1], grad_terms[2]), 'ctx')  223 us
    ppermute x4, waiting for transfers between devices, passed_along(): return lax.ppermute(block, axis, route)  102 us
    reshape x8, local copies, waits for them, and re-layouts, toeplitz_tiles(): return repeated.reshape(groups, rows_count, period - 1)[:, :, :cols_count]  76.8 us
    reshape x8, local copies, waits for them, and re-layouts, lag_totals(): flattened.reshape(groups, rows_count, cols_count + 1)  63.7 us
    all_gather x1, blocking collectives, body(): lax.all_gather(long_filter, 'fsdp', axis=1, tiled=True)  54.7 us
    unnamed x2, blocking collectives  48 us
    reduce_sum x3, other arithmetic, body(): short_parts.append(jnp.sum(grad_feat * earlier, axis=0))  43.3 us
    while x16, local copies, waits for them, and re-layouts  38.8 us
  transfers between devices with their start and end apart: 6, of which 3 were waited for; matrix products, arithmetic and copies ran while one was open for 14% of the time, Pallas kernels for 0%

commit v1 on v0

v1 whole, which is shorter than its diff:
```python
import functools

import jax
import jax.numpy as jnp
from jax import lax
from jax.experimental import pallas as pl
from jax.experimental.pallas import tpu as pltpu
from jax.sharding import PartitionSpec as P

C = 4096
GROUP = 16
LEN = 128
SHORT = 7
TOK = 128
TAIL = 16
LANES = 128
BLK = 512
SLABS = BLK // LANES
PER_SLAB = LANES // GROUP
BLOCKS = C // BLK
CHUNKS = ((0, 2), (2, 2), (4, 2), (6, 2))
FAR = 1 << 20
VMEM_LIMIT = 48 * 1024 * 1024

bf16 = jnp.bfloat16
f32 = jnp.float32


def ring(block, distance):
    count = lax.axis_size("ctx")
    return lax.ppermute(block, "ctx", [(i, (i + distance) % count) for i in range(count)])


def dot(a, b):
    return jnp.dot(a, b, preferred_element_type=f32)


def link_tables(listed):
    rows = jnp.arange(TOK, dtype=jnp.int32)
    usable = listed < TOK
    first = jnp.min(jnp.where(usable, listed, FAR))
    last = jnp.max(jnp.where(usable, listed, -FAR))
    latest = jnp.max(
        jnp.where(usable[None, :] & (listed[None, :] <= rows[:, None]), listed[None, :], -FAR), axis=1
    )
    t, s = rows[:, None], rows[None, :]
    own = (s <= t) & (latest[:, None] <= s)
    before = (s > t) & (t < first)
    own_t = (t <= s) & (latest[None, :] <= t)
    after_t = (t > s) & (t >= last)
    turned = s == TOK - 1 - t
    masks = jnp.stack([own, before, own_t, after_t, own[::-1], before[::-1], turned]).astype(bf16)
    lags = jnp.arange(1, SHORT, dtype=jnp.int32)[:, None, None]
    cols = jnp.arange(TAIL + TOK, dtype=jnp.int32)[None, None, :] - TAIL
    here = rows[None, :, None]
    shifts = (cols == here - lags) & (latest[None, :, None] <= here - lags)
    later = rows[None, None, :]
    unshifts = (later == here + lags) & (latest[None, None, :] <= here)
    shifts = shifts.astype(bf16).reshape((SHORT - 1) * TOK, TAIL + TOK)
    unshifts = unshifts.astype(bf16).reshape((SHORT - 1) * TOK, TOK)
    sends = jnp.stack([rows >= last, rows < first], axis=1).astype(f32)
    return masks, shifts, unshifts, sends, last, first


def short_sum(taps, near, moved):
    total = taps[0:1] * near
    for lag in range(1, SHORT):
        total = total + taps[lag : lag + 1] * moved[(lag - 1) * TOK : lag * TOK]
    return total


def feature_kernel(
    xq, xk, xv, tq, tk, tv, wq, wk, wv, grad_ref, shift_ref, send_ref,
    feat_ref, gate_ref, long_ref, gate_send_ref, long_send_ref,
):
    feats = []
    for place, (x, tail, taps) in enumerate(((xq, tq, wq), (xk, tk, wk), (xv, tv, wv))):
        own = x[...]
        moved = dot(shift_ref[...], jnp.concatenate([tail[...], own], axis=0))
        feat = short_sum(taps[0], own.astype(f32), moved)
        feat_ref[place] = feat
        feats.append(feat)
    gate = (feats[1] * feats[2]).astype(bf16)
    long_in = (grad_ref[...].astype(f32) * feats[0]).astype(bf16)
    gate_ref[...] = gate
    long_ref[...] = long_in
    gate_send_ref[...] = (gate.astype(f32) * send_ref[:, 0:1]).astype(bf16)
    long_send_ref[...] = (long_in.astype(f32) * send_ref[:, 1:2]).astype(bf16)


def feature_call(chunk, proj, tail, params, grad_out, shifts, sends, per_shard):
    base, count = chunk
    wide = count * BLK

    def cols(part):
        return lambda j: (0, part * BLOCKS + base + j)

    def taps(part):
        def index(j):
            place = part * BLOCKS + base + j
            return (place // per_shard, 0, place % per_shard)

        return index

    whole = lambda j: (0, 0)
    here = pl.BlockSpec((TOK, BLK), lambda j: (0, j))
    return pl.pallas_call(
        feature_kernel,
        grid=(count,),
        in_specs=[pl.BlockSpec((TOK, BLK), cols(part)) for part in range(3)]
        + [pl.BlockSpec((TAIL, BLK), cols(part)) for part in range(3)]
        + [pl.BlockSpec((1, 8, BLK), taps(part)) for part in range(3)]
        + [
            pl.BlockSpec((TOK, BLK), cols(0)),
            pl.BlockSpec(shifts.shape, whole),
            pl.BlockSpec(sends.shape, whole),
        ],
        out_specs=[pl.BlockSpec((3, TOK, BLK), lambda j: (0, 0, j)), here, here, here, here],
        out_shape=[jax.ShapeDtypeStruct((3, TOK, wide), f32)]
        + [jax.ShapeDtypeStruct((TOK, wide), bf16)] * 4,
        compiler_params=pltpu.CompilerParams(vmem_limit_bytes=VMEM_LIMIT),
        cost_estimate=pl.CostEstimate(
            flops=2 * 3 * 768 * 144 * wide, bytes_accessed=30 * TOK * wide, transcendentals=0
        ),
        name="features",
    )(proj, proj, proj, tail, tail, tail, params, params, params, grad_out, shifts, sends)


def main_kernel(
    feat_ref, gate_ref, long_ref, gate_halo_ref, long_halo_ref, grad_ref, x_ref, tail_ref, taps_ref,
    skip_ref, filt_ref, filt_back_ref, mask_ref, shift_ref, unshift_ref, send_ref, *rest,
):
    (mixed_ref, source_ref, short_ref, lag_ref, skip_grad_ref, head_ref, end_ref,
     ahead_ref, behind_ref, picked_ref, long_out_ref, gate_grad_ref, feat_grad_ref) = rest[-13:]
    part = pl.program_id(1)

    @pl.when(part == 0)
    def _():
        lane_group = lax.broadcasted_iota(jnp.int32, (TOK, LANES), 1) // GROUP

        def slab(step, carry):
            lanes = pl.ds(pl.multiple_of(step * LANES, LANES), LANES)
            gates = jnp.concatenate([gate_ref[:, lanes], gate_halo_ref[:, lanes]], axis=0)
            own_long = long_ref[:, lanes]
            longs = jnp.concatenate([own_long, long_halo_ref[:, lanes]], axis=0)
            turned = dot(mask_ref[6], own_long).astype(bf16)
            rows = pl.ds(pl.multiple_of(step * PER_SLAB, PER_SLAB), PER_SLAB)
            fore = filt_back_ref[rows, :]
            back = filt_ref[rows, :]
            for g in range(PER_SLAB):
                place = slice(g * TOK, (g + 1) * TOK)
                band = jnp.broadcast_to(fore[g : g + 1], (TOK, LANES))
                band = pltpu.roll(band, 0, 1, stride=1, stride_axis=0).astype(bf16)
                ahead_ref[place, :TOK] = band * mask_ref[0]
                ahead_ref[place, TOK:] = band * mask_ref[1]
                band = jnp.broadcast_to(back[g : g + 1], (TOK, LANES))
                band = pltpu.roll(band, 0, 1, stride=1, stride_axis=0).astype(bf16)
                behind_ref[place, :TOK] = band * mask_ref[2]
                behind_ref[place, TOK:] = band * mask_ref[3]
                picked_ref[place, :] = jnp.where(lane_group == g, turned, jnp.zeros_like(turned))
            forward = dot(ahead_ref[...], gates)
            backward = dot(behind_ref[...], longs)
            out = jnp.zeros((TOK, LANES), f32)
            spread = jnp.zeros((TOK, LANES), f32)
            for g in range(PER_SLAB):
                place = slice(g * TOK, (g + 1) * TOK)
                out = jnp.where(lane_group == g, forward[place], out)
                spread = jnp.where(lane_group == g, backward[place], spread)
            long_out_ref[:, lanes] = out
            gate_grad_ref[:, lanes] = spread
            product = lax.dot_general(
                picked_ref[...], gates, (((1,), (1,)), ((), ())), preferred_element_type=f32
            )
            own_mask = mask_ref[4].astype(f32)
            before_mask = mask_ref[5].astype(f32)
            sums = []
            for g in range(PER_SLAB):
                place = slice(g * TOK, (g + 1) * TOK)
                kept = product[place, :TOK] * own_mask + product[place, TOK:] * before_mask
                kept = pltpu.roll(kept, 0, 1, stride=1, stride_axis=0)
                sums.append(jnp.sum(kept, axis=0, keepdims=True))
            lag_ref[rows, :] = jnp.concatenate(sums, axis=0)
            return carry

        lax.fori_loop(0, SLABS, slab, 0)
        gate = gate_ref[...].astype(f32)
        upstream = grad_ref[...].astype(f32)
        query = feat_ref[0]
        skip = skip_ref[0, 7:8, :]
        combined = long_out_ref[...] + skip * gate
        through = upstream * query
        mixed_ref[...] = (query * combined).astype(bf16)
        feat_grad_ref[0] = upstream * combined
        gate_grad = gate_grad_ref[...] + skip * through
        feat_grad_ref[1] = gate_grad * feat_ref[2]
        feat_grad_ref[2] = gate_grad * feat_ref[1]
        skip_grad = jnp.sum(through * gate, axis=0, keepdims=True)
        for k in range(SLABS):
            skip_grad_ref[k] = skip_grad[:, k * LANES : (k + 1) * LANES]

    feat_grad = feat_grad_ref[part]
    own = x_ref[...]
    moved = dot(shift_ref[...], jnp.concatenate([tail_ref[...], own], axis=0))
    near = own.astype(f32)
    sums = [jnp.sum(feat_grad * near, axis=0, keepdims=True)]
    for lag in range(1, SHORT):
        sums.append(
            jnp.sum(feat_grad * moved[(lag - 1) * TOK : lag * TOK], axis=0, keepdims=True)
        )
    sums.append(jnp.zeros_like(sums[0]))
    sums = jnp.concatenate(sums, axis=0)
    for k in range(SLABS):
        short_ref[k] = sums[:, k * LANES : (k + 1) * LANES]
    source = short_sum(taps_ref[0], feat_grad, dot(unshift_ref[...], feat_grad.astype(bf16)))
    source_ref[...] = source.astype(bf16)
    end_ref[...] = source[TOK - 8 :]
    head_ref[...] = (feat_grad[:TAIL] * send_ref[:TAIL, 1:2]).astype(bf16)


def main_call(chunk, feats, gates, longs, gate_halo, long_halo, grad_out, proj, tail, params,
              filt, filt_back, masks, shifts, unshifts, sends, per_shard, kept):
    base, count = chunk
    shards = params.shape[0]
    skip_blocks = BLOCKS // shards
    local = pl.BlockSpec((TOK, BLK), lambda j, p: (0, j))
    first_cols = pl.BlockSpec((TOK, BLK), lambda j, p: (0, base + j))

    def cols(rows):
        return pl.BlockSpec((rows, BLK), lambda j, p: (0, p * BLOCKS + base + j))

    def taps(j, p):
        place = p * BLOCKS + base + j
        return (place // per_shard, 0, place % per_shard)

    def skips(j, p):
        return ((base + j) // skip_blocks, 0, (base + j) % skip_blocks)

    def whole(array):
        return pl.BlockSpec(array.shape, lambda j, p: (0,) * array.ndim)

    groups = BLK // GROUP
    filt_spec = pl.BlockSpec((groups, LEN), lambda j, p: (base + j, 0))
    operands = [feats, gates, longs, gate_halo, long_halo, grad_out, proj, tail, params, params,
                filt, filt_back, masks, shifts, unshifts, sends]
    in_specs = [
        pl.BlockSpec((3, TOK, BLK), lambda j, p: (0, 0, j)), local, local, local, local, first_cols,
        cols(TOK), cols(TAIL), pl.BlockSpec((1, 8, BLK), taps), pl.BlockSpec((1, 8, BLK), skips),
        filt_spec, filt_spec, whole(masks), whole(shifts), whole(unshifts), whole(sends),
    ]
    aliases = {}
    if kept is not None:
        aliases = {len(operands) + k: k for k in range(len(kept))}
        operands = operands + list(kept)
        in_specs = in_specs + [pl.BlockSpec(memory_space=pl.ANY)] * len(kept)
    slabs = C // LANES
    return pl.pallas_call(
        main_kernel,
        grid=(count, 3),
        in_specs=in_specs,
        out_specs=[
            first_cols, cols(TOK),
            pl.BlockSpec((SLABS, 8, LANES), lambda j, p: (p * BLOCKS + base + j, 0, 0)),
            pl.BlockSpec((groups, LANES), lambda j, p: (base + j, 0)),
            pl.BlockSpec((SLABS, 1, LANES), lambda j, p: (base + j, 0, 0)),
            cols(TAIL), cols(8),
        ],
        out_shape=[
            jax.ShapeDtypeStruct((TOK, C), bf16),
            jax.ShapeDtypeStruct((TOK, 3 * C), bf16),
            jax.ShapeDtypeStruct((3 * slabs, 8, LANES), f32),
            jax.ShapeDtypeStruct((C // GROUP, LANES), f32),
            jax.ShapeDtypeStruct((slabs, 1, LANES), f32),
            jax.ShapeDtypeStruct((TAIL, 3 * C), bf16),
            jax.ShapeDtypeStruct((8, 3 * C), f32),
        ],
        scratch_shapes=[
            pltpu.VMEM((PER_SLAB * TOK, 2 * TOK), bf16),
            pltpu.VMEM((PER_SLAB * TOK, 2 * TOK), bf16),
            pltpu.VMEM((PER_SLAB * TOK, LANES), bf16),
            pltpu.VMEM((TOK, BLK), f32),
            pltpu.VMEM((TOK, BLK), f32),
            pltpu.VMEM((3, TOK, BLK), f32),
        ],
        input_output_aliases=aliases,
        compiler_params=pltpu.CompilerParams(vmem_limit_bytes=VMEM_LIMIT),
        cost_estimate=pl.CostEstimate(
            flops=20_000_000_000 * count, bytes_accessed=40 * TOK * count * BLK, transcendentals=0
        ),
        name="main",
    )(*operands)


def patch_kernel(source_ref, end_ref, head_ref, taps_ref, keep_ref, out_ref):
    ahead = jnp.concatenate([jnp.zeros((8, head_ref.shape[1]), f32), head_ref[...].astype(f32)[:8]], axis=0)
    extra = jnp.zeros((8, head_ref.shape[1]), f32)
    taps = taps_ref[0]
    for lag in range(1, SHORT):
        extra = extra + taps[lag : lag + 1] * ahead[lag : lag + 8]
    final = end_ref[...] + extra * keep_ref[...]
    out_ref[...] = jnp.concatenate([source_ref[...].astype(f32)[:8], final], axis=0).astype(bf16)


def patch_call(source, end, head, params, keep):
    wide = params.shape[2]
    rows = TOK // TAIL - 1
    return pl.pallas_call(
        patch_kernel,
        grid=(3 * C // wide,),
        in_specs=[
            pl.BlockSpec((TAIL, wide), lambda j: (rows, j)),
            pl.BlockSpec((8, wide), lambda j: (0, j)),
            pl.BlockSpec((TAIL, wide), lambda j: (0, j)),
            pl.BlockSpec((1, 8, wide), lambda j: (j, 0, 0)),
            pl.BlockSpec((8, 1), lambda j: (0, 0)),
        ],
        out_specs=pl.BlockSpec((TAIL, wide), lambda j: (rows, j)),
        out_shape=jax.ShapeDtypeStruct(source.shape, bf16),
        input_output_aliases={0: 0},
        name="patch",
    )(source, end, head, params, keep)


def body(proj, short_taps, long_filter, skip, grad_out, starts):
    shards, count = lax.axis_size("fsdp"), lax.axis_size("ctx")
    source, upstream = proj[0], grad_out[0]
    masks, shifts, unshifts, sends, last, _ = link_tables(starts[0, 0])
    rows = jnp.arange(TOK - 8, TOK, dtype=jnp.int32)[:, None]
    tail = jnp.where(rows >= last, source[TOK - 8 :], jnp.zeros((), bf16))
    tail = jnp.pad(ring(tail, 1), ((TAIL - 8, 0), (0, 0)))
    wide = short_taps.shape[1]
    filt_rows = -(-long_filter.size // wide)
    flat = jnp.pad(long_filter.T.reshape(-1), (0, filt_rows * wide - long_filter.size))
    packed = jnp.concatenate(
        [short_taps, jnp.pad(skip, (0, wide - skip.shape[0]))[None], flat.reshape(filt_rows, wide)]
    )
    params = lax.all_to_all(
        jnp.broadcast_to(packed[None], (shards,) + packed.shape), "fsdp", 0, 0, tiled=True
    )
    filt = params[:, 8:].reshape(shards, -1)[:, : long_filter.size].reshape(C // GROUP, LEN)
    filt = filt.astype(bf16).astype(f32)
    filt_back = jnp.roll(filt[:, ::-1], 1, axis=1)
    per_shard = wide // BLK

    parts = []
    for chunk in CHUNKS:
        feats, gates, longs, gate_send, long_send = feature_call(
            chunk, source, tail, params, upstream, shifts, sends, per_shard
        )
        parts.append((feats, gates, longs, ring(gate_send, 1), ring(long_send, -1)))
    kept = None
    for chunk, part in zip(CHUNKS, parts):
        kept = main_call(
            chunk, *part, upstream, source, tail, params, filt, filt_back, masks, shifts, unshifts,
            sends, per_shard, kept,
        )
    mixed, grad_source, short_sums, lag_sums, skip_sums, head, end = kept
    head = ring(head, -1)

    short_sums = short_sums.reshape(shards, -1, 8, LANES)
    skip_slabs = C // LANES // shards
    short_sums = short_sums.at[:, :skip_slabs, 7].set(skip_sums.reshape(shards, skip_slabs, LANES))
    sums = jnp.concatenate(
        [short_sums.reshape(shards, -1, LANES), lag_sums.reshape(shards, -1, LANES)], axis=1
    )
    piece = sums.shape[1] // count
    sums = sums.reshape(shards * count, piece, LANES)
    sums = jnp.sum(lax.all_to_all(sums, ("fsdp", "ctx"), 0, 0, tiled=True), axis=0)
    sums = sums * (float(shards * count * TOK) ** -0.5)
    sums = lax.all_to_all(
        jnp.broadcast_to(sums[None], (count,) + sums.shape), "ctx", 0, 0, tiled=True
    ).reshape(count * piece, LANES)
    slabs = 3 * C // LANES // shards
    grad_short = sums[: slabs * 8].reshape(slabs, 8, LANES)
    grad_skip = grad_short[:skip_slabs, 7].reshape(-1)
    grad_short = grad_short[:, :SHORT].transpose(1, 0, 2).reshape(SHORT, -1)
    grad_long = sums[slabs * 8 :, ::-1].T

    keep = (rows >= last).astype(f32)
    grad_source = patch_call(grad_source, end, head, params, keep)
    return mixed[None], grad_source[None], grad_short, grad_long, grad_skip


def solution(mesh):
    placed = (
        P("fsdp", "ctx", None),
        P(None, "fsdp"),
        P(None, "fsdp"),
        P("fsdp"),
        P("fsdp", "ctx", None),
        P("fsdp", "ctx", None),
    )
    return jax.shard_map(
        body,
        mesh=mesh,
        in_specs=placed,
        out_specs=(
            P("fsdp", "ctx", None),
            P("fsdp", "ctx", None),
            P(None, "fsdp"),
            P(None, "fsdp"),
            P("fsdp"),
        ),
        check_vma=False,
    )
```

time: 1030 us -> 232 us (0.23)
  blocking collectives: 353 us -> 0 us
  local copies, waits for them, and re-layouts: 292 us -> 23.1 us
  other arithmetic: 160 us -> 13.7 us
  waiting for transfers between devices: 110 us -> 36.8 us
  starting transfers between devices: 14.4 us -> 86.8 us
  Pallas kernels: 0 us -> 69.2 us
  matrix products: 61.7 us -> 0 us
  loops' own time: 21.4 us -> 0 us
  between operations: 16.4 us -> 1.01 us
    psum x1 -> x0, blocking collectives: 223 us -> none  [body(): summed = lax.psum((grad_terms[0], grad_terms[1], grad_terms[2]), 'ctx')]
    reshape x16 -> x2, local copies, waits for them, and re-layouts: 141 us -> 0.64 us  [the longest x1 0.63 us: body(): grad_short = grad_short[:, :SHORT].transpose(1, 0, 2).reshape(SHORT, -1)]
    ppermute x4 -> x10, waiting for transfers between devices: 102 us -> 10.3 us  [ring(): lax.ppermute(block, 'ctx', [(i, (i + distance) % count) for i in range(co...]
    all_gather x3 -> x0, blocking collectives: 81.2 us -> none  [the longest x1 54.7 us: body(): lax.all_gather(long_filter, 'fsdp', axis=1, tiled=True)]
    reduce_sum x12 -> x1, other arithmetic: 71.2 us -> 0.28 us  [body(): jnp.sum(lax.all_to_all(sums, ('fsdp', 'ctx'), 0, 0, tiled=True), axis=0)]
    pallas_call x0 -> x9, Pallas kernels: none -> 69.2 us  [the longest x4 51.2 us: main_call(): pl.pallas_call(main_kernel, grid=(count, 3), in_specs=in_specs, out_specs...]
    dot_general x24 -> x0, matrix products: 61.7 us -> none  [the longest x8 24.4 us: joint_block(): jnp.einsum('gcs,gts->gct', win_blk, tiles, preferred_element_type=jnp.flo...]
    add x2, other arithmetic: 50.8 us -> 0.07 us  [the longest x1 0.07 us: link_tables(): unshifts = (later == here + lags) & (latest[None, None, :] <= here)]
  transfers between devices with their start and end apart: 6 -> 13, of which waited for: 3 -> 6; matrix products, arithmetic and copies ran while one was open for 14% -> 6% of each run, Pallas kernels for 0% -> 23%
where the time goes in v1:
time: 232 us; the launch traced here: 231 us
  starting transfers between devices  86.8 us (37%)
  Pallas kernels  69.2 us (30%)
  waiting for transfers between devices  36.8 us (16%)
  local copies, waits for them, and re-layouts  23.1 us (10%)
  other arithmetic  13.7 us (6%)
    pallas_call x4, Pallas kernels, main_call(): pl.pallas_call(main_kernel, grid=(count, 3), in_specs=in_specs, out_specs...  51.2 us
    ppermute x10, starting transfers between devices, ring(): lax.ppermute(block, 'ctx', [(i, (i + distance) % count) for i in range(co...  49.5 us
    all_to_all x1, starting transfers between devices, body(): lax.all_to_all(jnp.broadcast_to(sums[None], (count,) + sums.shape), 'ctx'...  21.1 us
    unnamed x54, local copies, waits for them, and re-layouts  12.9 us
    pallas_call x4, Pallas kernels, feature_call(): pl.pallas_call(feature_kernel, grid=(count,), in_specs=[pl.BlockSpec((TOK...  12.8 us
    all_to_all x1, starting transfers between devices, body(): lax.all_to_all(sums, ('fsdp', 'ctx'), 0, 0, tiled=True)  11.7 us
    all_to_all x1, waiting for transfers between devices, body(): lax.all_to_all(jnp.broadcast_to(packed[None], (shards,) + packed.shape),...  11.2 us
    ppermute x10, waiting for transfers between devices, ring(): lax.ppermute(block, 'ctx', [(i, (i + distance) % count) for i in range(co...  10.3 us
  transfers between devices with their start and end apart: 13, of which 6 were waited for; matrix products, arithmetic and copies ran while one was open for 6% of the time, Pallas kernels for 23%

profile of v1, /device:TPU:32, one launch (start us, length us, event | category | flops | bytes accessed | tf_op | source)
XLA Modules:
  0.0 230.6 jit_solution(10543427655400869913)
XLA Ops:
  0.7 1.4 select_reduce_fusion.1
  2.1 0.7 add_compare_fusion.1
  2.7 1.0 bitcast_select_fusion
  3.7 6.4 %collective-permute-start = (bf16[8,12288]{1,0:T(8,128)(2,1)S(1)}, bf16[8,12288]{1,0:T(8,128)(2,1)S(1)}, u32[]{:S(2)}, u32[]{:S(2)}) collective-permute-start(bf16[8,12288]{1,0:T(8,128)(2,1)S(1)} %bitcast_select_fusion), channel_id=1, source_target_pairs={{0,8},{8,16},{16,24},{24,32},{32,40},{40,48},{48,56},{56,64},{64,7... | collective-permute-start | bytes 589832 | tf_op jit(solution)/shard_map/ppermute | solution.py:31
  10.1 0.7 pad.18
  10.8 0.7 pad.17
  11.5 0.8 pad_maximum_fusion.2
  12.3 1.0 broadcast_in_dim.67
  13.3 4.5 %all-to-all-start = ((f32[8,11,1536]{2,1,0:T(8,128)}), f32[8,11,1536]{2,1,0:T(8,128)S(1)}, u32[]{:S(2)}, u32[]{:S(2)}) async-start(f32[8,11,1536]{2,1,0:T(8,128)} %broadcast_in_dim.67), calls=%async_computation | async-start | bytes 1572864 | tf_op jit(solution)/shard_map/all_to_all | solution.py:336
  17.8 0.7 broadcast_compare_fusion
  18.4 1.3 iota_compare_fusion.15
  19.7 1.3 iota_compare_fusion.13
  22.1 0.8 fusion.1.unshift_ref
  23.0 0.6 fusion.16
  23.6 0.7 and_reduce_fusion
  24.7 11.2 %all-to-all-done.wq.wk.wv.taps_ref.skip_ref = f32[8,11,1536]{2,1,0:T(8,128)S(1)} async-done(((f32[8,11,1536]{2,1,0:T(8,128)}), f32[8,11,1536]{2,1,0:T(8,128)S(1)}, u32[]{:S(2)}, u32[]{:S(2)}) %all-to-all-start) | async-done | bytes 540704 | tf_op jit(solution)/shard_map/all_to_all | solution.py:336
  35.9 3.9 %features.7 = (f32[3,128,1024]{2,1,0:T(8,128)S(1)}, bf16[128,1024]{1,0:T(8,128)(2,1)S(1)}, bf16[128,1024]{1,0:T(8,128)(2,1)S(1)}, bf16[128,1024]{1,0:T(8,128)(2,1)}, bf16[128,1024]{1,0:T(8,128)(2,1)}) custom-call(bf16[128,12288]{1,0:T(8,128)(2,1)} %bitcast.65, bf16[128,12288]{1,0:T(8,128)(2,1)} %bitcast.66, bf16[128,12288]{1,0:T(8,128)(2,1)} %bitcast.67, ...), custom_call_target="tpu_custom_call" | custom-call | flops 679477248 | bytes 3932160 | tf_op jit(solution)/shard_map/features/pallas_call | solution.py:107
  39.7 1.2 copy-done.8
  40.9 0.8 copy-done.16
  41.6 4.3 %collective-permute-start.7 = (bf16[128,1024]{1,0:T(8,128)(2,1)}, bf16[128,1024]{1,0:T(8,128)(2,1)S(1)}, u32[]{:S(2)}, u32[]{:S(2)}) collective-permute-start(bf16[128,1024]{1,0:T(8,128)(2,1)} %get-tuple-element.83), channel_id=1, source_target_pairs={{0,8},{8,16},{16,24},{24,32},{32,40},{40,48},{48,56},{56,64},{64,7... | collective-permute-start | bytes 786440 | tf_op jit(solution)/shard_map/ppermute | solution.py:31
  45.9 5.8 %collective-permute-start.8 = (bf16[128,1024]{1,0:T(8,128)(2,1)}, bf16[128,1024]{1,0:T(8,128)(2,1)}, u32[]{:S(2)}, u32[]{:S(2)}) collective-permute-start(bf16[128,1024]{1,0:T(8,128)(2,1)} %get-tuple-element.84), channel_id=1, source_target_pairs={{0,248},{8,0},{16,8},{24,16},{32,24},{40,32},{48,40},{56,48},{64,5... | collective-permute-start | bytes 786440 | tf_op jit(solution)/shard_map/ppermute | solution.py:31
  51.9 3.0 %features.6 = (f32[3,128,1024]{2,1,0:T(8,128)S(1)}, bf16[128,1024]{1,0:T(8,128)(2,1)S(1)}, bf16[128,1024]{1,0:T(8,128)(2,1)S(1)}, bf16[128,1024]{1,0:T(8,128)(2,1)S(1)}, bf16[128,1024]{1,0:T(8,128)(2,1)S(1)}) custom-call(bf16[128,12288]{1,0:T(8,128)(2,1)} %bitcast.68, bf16[128,12288]{1,0:T(8,128)(2,1)} %bitcast.69, bf16[128,12288]{1,0:T(8,128)(2,1)} %bitcast.70, ...), custom_call_target="tpu_custom_call" | custom-call | flops 679477248 | bytes 3932160 | tf_op jit(solution)/shard_map/features/pallas_call | solution.py:107
  54.9 1.2 copy-done.7
  56.0 0.7 copy-done.10
  56.7 0.7 copy-done.12
  57.4 0.7 copy-done.20
  58.1 0.7 copy-done.21
  58.9 0.8 slice.93
  59.7 1.0 slice.82
  60.8 10.1 %collective-permute-start.6 = (bf16[128,1024]{1,0:T(8,128)(2,1)}, bf16[128,1024]{1,0:T(8,128)(2,1)S(1)}, u32[]{:S(2)}, u32[]{:S(2)}) collective-permute-start(bf16[128,1024]{1,0:T(8,128)(2,1)} %copy-done.20), channel_id=1, source_target_pairs={{0,248},{8,0},{16,8},{24,16},{32,24},{40,32},{48,40},{56,48},{64,5... | collective-permute-start | bytes 786440 | tf_op jit(solution)/shard_map/ppermute | solution.py:31
  70.9 2.9 %features.5 = (f32[3,128,1024]{2,1,0:T(8,128)S(1)}, bf16[128,1024]{1,0:T(8,128)(2,1)S(1)}, bf16[128,1024]{1,0:T(8,128)(2,1)S(1)}, bf16[128,1024]{1,0:T(8,128)(2,1)S(1)}, bf16[128,1024]{1,0:T(8,128)(2,1)S(1)}) custom-call(bf16[128,12288]{1,0:T(8,128)(2,1)} %bitcast.71, bf16[128,12288]{1,0:T(8,128)(2,1)} %bitcast.72, bf16[128,12288]{1,0:T(8,128)(2,1)} %bitcast.73, ...), custom_call_target="tpu_custom_call" | custom-call | flops 679477248 | bytes 3932160 | tf_op jit(solution)/shard_map/features/pallas_call | solution.py:107
  73.8 1.2 copy-done.6
  75.1 3.0 %features.4 = (f32[3,128,1024]{2,1,0:T(8,128)S(1)}, bf16[128,1024]{1,0:T(8,128)(2,1)S(1)}, bf16[128,1024]{1,0:T(8,128)(2,1)S(1)}, bf16[128,1024]{1,0:T(8,128)(2,1)S(1)}, bf16[128,1024]{1,0:T(8,128)(2,1)S(1)}) custom-call(bf16[128,12288]{1,0:T(8,128)(2,1)} %bitcast.74, bf16[128,12288]{1,0:T(8,128)(2,1)} %bitcast.75, bf16[128,12288]{1,0:T(8,128)(2,1)} %bitcast.76, ...), custom_call_target="tpu_custom_call" | custom-call | flops 679477248 | bytes 3932160 | tf_op jit(solution)/shard_map/features/pallas_call | solution.py:107
  78.1 1.1 copy-done.5
  79.4 0.7 copy-done.18
  80.1 10.0 %collective-permute-start.4 = (bf16[128,1024]{1,0:T(8,128)(2,1)S(1)}, bf16[128,1024]{1,0:T(8,128)(2,1)S(1)}, u32[]{:S(2)}, u32[]{:S(2)}) collective-permute-start(bf16[128,1024]{1,0:T(8,128)(2,1)S(1)} %get-tuple-element.74), channel_id=1, source_target_pairs={{0,248},{8,0},{16,8},{24,16},{32,24},{40,32},{48,40},{56,48},{64,5... | collective-permute-start | bytes 786440 | tf_op jit(solution)/shard_map/ppermute | solution.py:31
  90.2 0.9 copy-done.19
  91.1 12.9 %main.4 = (bf16[128,4096]{1,0:T(8,128)(2,1)}, bf16[128,12288]{1,0:T(8,128)(2,1)}, f32[96,8,128]{2,1,0:T(8,128)S(1)}, f32[256,128]{1,0:T(8,128)S(1)}, f32[32,1,12...) custom-call(f32[3,128,1024]{2,1,0:T(8,128)} %copy-done.8, bf16[128,1024]{1,0:T(8,128)(2,1)S(1)} %copy-done.15, ...), custom_call_target="tpu_custom_call" | custom-call | flops 40000000000 | bytes 5242880 | tf_op jit(solution)/shard_map/main/pallas_call | solution.py:256
  104.0 7.7 %collective-permute-done.5.gate_halo_ref = bf16[128,1024]{1,0:T(8,128)(2,1)S(1)} collective-permute-done((bf16[128,1024]{1,0:T(8,128)(2,1)}, bf16[128,1024]{1,0:T(8,128)(2,1)S(1)}, u32[]{:S(2)}, u32[]{:S(2)}) %collective-permute-start.5) | collective-permute-done | bytes 262176 | tf_op jit(solution)/shard_map/ppermute | solution.py:31
  111.7 2.6 %collective-permute-start.2 = (bf16[128,1024]{1,0:T(8,128)(2,1)S(1)}, bf16[128,1024]{1,0:T(8,128)(2,1)S(1)}, u32[]{:S(2)}, u32[]{:S(2)}) collective-permute-start(bf16[128,1024]{1,0:T(8,128)(2,1)S(1)} %get-tuple-element.69), channel_id=1, source_target_pairs={{0,248},{8,0},{16,8},{24,16},{32,24},{40,32},{48,40},{56,48},{64,5... | collective-permute-start | bytes 786440 | tf_op jit(solution)/shard_map/ppermute | solution.py:31
  114.3 12.8 %main.5 = (bf16[128,4096]{1,0:T(8,128)(2,1)}, bf16[128,12288]{1,0:T(8,128)(2,1)}, f32[96,8,128]{2,1,0:T(8,128)S(1)}, f32[256,128]{1,0:T(8,128)S(1)}, f32[32,1,12...) custom-call(f32[3,128,1024]{2,1,0:T(8,128)} %copy-done.7, ...), custom_call_target="tpu_custom_call", output_to_operand_aliasing={{0}: (16, {}), {1}: (17, {}), {2}: (18, {}), {3}: (19, {}),... | custom-call | flops 40000000000 | bytes 5242880 | tf_op jit(solution)/shard_map/main/pallas_call | solution.py:256
  127.2 12.7 %main.6 = (bf16[128,4096]{1,0:T(8,128)(2,1)}, bf16[128,12288]{1,0:T(8,128)(2,1)}, f32[96,8,128]{2,1,0:T(8,128)S(1)}, f32[256,128]{1,0:T(8,128)S(1)}, f32[32,1,12...) custom-call(f32[3,128,1024]{2,1,0:T(8,128)} %copy-done.6, ...), custom_call_target="tpu_custom_call", output_to_operand_aliasing={{0}: (16, {}), {1}: (17, {}), {2}: (18, {}), {3}: (19, {}),... | custom-call | flops 40000000000 | bytes 5242880 | tf_op jit(solution)/shard_map/main/pallas_call | solution.py:256
  140.0 2.4 %collective-permute-done.2.long_halo_ref = bf16[128,1024]{1,0:T(8,128)(2,1)S(1)} collective-permute-done((bf16[128,1024]{1,0:T(8,128)(2,1)S(1)}, bf16[128,1024]{1,0:T(8,128)(2,1)S(1)}, u32[]{:S(2)}, u32[]{:S(2)}) %collective-permute-start.2) | collective-permute-done | bytes 262176 | tf_op jit(solution)/shard_map/ppermute | solution.py:31
  142.4 12.7 %main.7 = (bf16[128,4096]{1,0:T(8,128)(2,1)}, bf16[128,12288]{1,0:T(8,128)(2,1)}, f32[96,8,128]{2,1,0:T(8,128)S(1)}, f32[256,128]{1,0:T(8,128)S(1)}, f32[32,1,12...) custom-call(f32[3,128,1024]{2,1,0:T(8,128)} %copy-done.5, ...), custom_call_target="tpu_custom_call", output_to_operand_aliasing={{0}: (16, {}), {1}: (17, {}), {2}: (18, {}), {3}: (19, {}),... | custom-call | flops 40000000000 | bytes 5242880 | tf_op jit(solution)/shard_map/main/pallas_call | solution.py:256
  155.2 0.8 copy-done.2
  155.9 0.7 copy-done.4
  156.6 0.7 copy-done.9
  157.3 1.3 constant_dynamic-slice_fusion
  158.6 0.5 broadcast_select_fusion
  159.2 1.4 scatter.4
  160.6 1.7 pad_maximum_fusion
  162.3 11.7 %all-to-all-start.1 = ((f32[256,4,128]{2,1,0:T(4,128)}), f32[256,4,128]{2,1,0:T(4,128)S(1)}, u32[]{:S(2)}, u32[]{:S(2)}) async-start(f32[256,4,128]{2,1,0:T(4,128)} %bitcast.20), calls=%async_computation.1 | async-start | bytes 1048576 | tf_op jit(solution)/shard_map/all_to_all | solution.py:367
  174.1 10.1 %collective-permute-start.9 = (bf16[16,12288]{1,0:T(8,128)(2,1)}, bf16[16,12288]{1,0:T(8,128)(2,1)S(1)}, u32[]{:S(2)}, u32[]{:S(2)}) collective-permute-start(bf16[16,12288]{1,0:T(8,128)(2,1)} %copy-done.9), channel_id=1, source_target_pairs={{0,248},{8,0},{16,8},{24,16},{32,24},{40,32},{48,40},{56,48},{64,5... | collective-permute-start | bytes 1179656 | tf_op jit(solution)/shard_map/ppermute | solution.py:31
  184.2 10.2 %all-to-all-done.1 = f32[256,4,128]{2,1,0:T(4,128)S(1)} async-done(((f32[256,4,128]{2,1,0:T(4,128)}), f32[256,4,128]{2,1,0:T(4,128)S(1)}, u32[]{:S(2)}, u32[]{:S(2)}) %all-to-all-start.1) | async-done | bytes 524320 | tf_op jit(solution)/shard_map/all_to_all | solution.py:367
  194.4 0.3 reduce_sum.9
  194.7 0.6 broadcast_in_dim.72
  195.3 21.1 %all-to-all-start.2 = ((f32[32,4,128]{2,1,0:T(4,128)}), f32[32,4,128]{2,1,0:T(4,128)S(1)}, u32[]{:S(2)}, u32[]{:S(2)}) async-start(f32[32,4,128]{2,1,0:T(4,128)} %broadcast_in_dim.72), calls=%async_computation.2 | async-start | bytes 131072 | tf_op jit(solution)/shard_map/all_to_all | solution.py:369
  216.4 1.2 fusion.14.keep_ref
  217.7 0.7 copy-done.22
  218.4 5.2 %patch.1 = bf16[128,12288]{1,0:T(8,128)(2,1)} custom-call(bf16[128,12288]{1,0:T(8,128)(2,1)} %get-tuple-element.107.source_ref, f32[8,12288]{1,0:T(8,128)} %copy-done.2, bf16[16,12288]{1,0:T(8,128)(2,1)} %copy-done.22, f32[8,11,1536]{2,1,0:T(8,128)} %copy-done, f32[8,1]{1,0:T(8,128)} %fusion.14.keep_ref), custom_call_target="tpu_custom_call", output_to_operand_aliasing={{}: (0, {})} | custom-call | tf_op jit(solution)/shard_map/patch/pallas_call | solution.py:306
  223.6 5.1 %all-to-all-done.2 = f32[32,4,128]{2,1,0:T(4,128)S(1)} async-done(((f32[32,4,128]{2,1,0:T(4,128)}), f32[32,4,128]{2,1,0:T(4,128)S(1)}, u32[]{:S(2)}, u32[]{:S(2)}) %all-to-all-start.2) | async-done | bytes 65568 | tf_op jit(solution)/shard_map/all_to_all | solution.py:369
  228.7 0.6 slice_bitcast_fusion
  229.3 0.6 slice.97
  229.9 0.7 rev.12
  (81 shorter events, 2.0 us)
Async XLA Ops:
  0.6 23.0 %copy-start.23 = (s32[4]{0:T(128)S(1)}, s32[4]{0:T(128)}, u32[]{:S(2)}) copy-start(s32[4]{0:T(128)} %constant.53.clone.1) | copy-start | bytes 52
  0.6 20.4 %copy-start.24 = (s32[1,1,4]{2,1,0:T(1,128)S(1)}, s32[1,1,4]{2,1,0:T(1,128)}, u32[]{:S(2)}) copy-start(s32[1,1,4]{2,1,0:T(1,128)} %param.13) | copy-start | bytes 52
  0.7 35.2 %copy-start.1 = (bf16[1,128,4096]{2,1,0:T(8,128)(2,1)S(1)}, bf16[1,128,4096]{2,1,0:T(8,128)(2,1)}, u32[]{:S(2)}) copy-start(bf16[1,128,4096]{2,1,0:T(8,128)(2,1)} %param.12) | copy-start | bytes 3145732
  3.7 20.9 %collective-permute-start = (bf16[8,12288]{1,0:T(8,128)(2,1)S(1)}, bf16[8,12288]{1,0:T(8,128)(2,1)S(1)}, u32[]{:S(2)}, u32[]{:S(2)}) collective-permute-start(bf16[8,12288]{1,0:T(8,128)(2,1)S(1)} %bitcast_select_fusion), channel_id=1, source_target_pairs={{0,8},{8,16},{16,24},{24,32},{32,40},{40,48},{48,56},{56,64},{64,7... | collective-permute-start | bytes 589832 | tf_op jit(solution)/shard_map/ppermute | solution.py:31
  13.3 22.6 %all-to-all-start = ((f32[8,11,1536]{2,1,0:T(8,128)}), f32[8,11,1536]{2,1,0:T(8,128)S(1)}, u32[]{:S(2)}, u32[]{:S(2)}) async-start(f32[8,11,1536]{2,1,0:T(8,128)} %broadcast_in_dim.67), calls=%async_computation | async-start | bytes 1572864 | tf_op jit(solution)/shard_map/all_to_all | solution.py:336
  35.9 106.5 %copy-start = (f32[8,11,1536]{2,1,0:T(8,128)}, f32[8,11,1536]{2,1,0:T(8,128)S(1)}, u32[]{:S(2)}) copy-start(f32[8,11,1536]{2,1,0:T(8,128)S(1)} %all-to-all-done.wq.wk.wv.taps_ref.skip_ref) | copy-start | bytes 1622020
  39.7 1.2 copy-start.8
  40.9 0.8 copy-start.16
  41.6 10.2 %copy-start.14 = (bf16[128,1024]{1,0:T(8,128)(2,1)}, bf16[128,1024]{1,0:T(8,128)(2,1)S(1)}, u32[]{:S(2)}) copy-start(bf16[128,1024]{1,0:T(8,128)(2,1)S(1)} %get-tuple-element.81.gate_ref) | copy-start | bytes 786436
  41.6 37.7 %collective-permute-start.7 = (bf16[128,1024]{1,0:T(8,128)(2,1)}, bf16[128,1024]{1,0:T(8,128)(2,1)S(1)}, u32[]{:S(2)}, u32[]{:S(2)}) collective-permute-start(bf16[128,1024]{1,0:T(8,128)(2,1)} %get-tuple-element.83), channel_id=1, source_target_pairs={{0,8},{8,16},{16,24},{24,32},{32,40},{40,48},{48,56},{56,64},{64,7... | collective-permute-start | bytes 786440 | tf_op jit(solution)/shard_map/ppermute | solution.py:31
  45.9 44.2 %collective-permute-start.8 = (bf16[128,1024]{1,0:T(8,128)(2,1)}, bf16[128,1024]{1,0:T(8,128)(2,1)}, u32[]{:S(2)}, u32[]{:S(2)}) collective-permute-start(bf16[128,1024]{1,0:T(8,128)(2,1)} %get-tuple-element.84), channel_id=1, source_target_pairs={{0,248},{8,0},{16,8},{24,16},{32,24},{40,32},{48,40},{56,48},{64,5... | collective-permute-start | bytes 786440 | tf_op jit(solution)/shard_map/ppermute | solution.py:31
  54.9 1.2 copy-start.7
  56.0 0.7 copy-start.10
  56.7 0.7 copy-start.12
  57.4 0.7 copy-start.20
  58.1 0.7 copy-start.21
  60.7 51.1 %collective-permute-start.5 = (bf16[128,1024]{1,0:T(8,128)(2,1)}, bf16[128,1024]{1,0:T(8,128)(2,1)S(1)}, u32[]{:S(2)}, u32[]{:S(2)}) collective-permute-start(bf16[128,1024]{1,0:T(8,128)(2,1)} %copy-done.21), channel_id=1, source_target_pairs={{0,8},{8,16},{16,24},{24,32},{32,40},{40,48},{48,56},{56,64},{64,7... | collective-permute-start | bytes 786440 | tf_op jit(solution)/shard_map/ppermute | solution.py:31
  60.8 53.5 %collective-permute-start.6 = (bf16[128,1024]{1,0:T(8,128)(2,1)}, bf16[128,1024]{1,0:T(8,128)(2,1)S(1)}, u32[]{:S(2)}, u32[]{:S(2)}) collective-permute-start(bf16[128,1024]{1,0:T(8,128)(2,1)} %copy-done.20), channel_id=1, source_target_pairs={{0,248},{8,0},{16,8},{24,16},{32,24},{40,32},{48,40},{56,48},{64,5... | collective-permute-start | bytes 786440 | tf_op jit(solution)/shard_map/ppermute | solution.py:31
  73.8 1.2 copy-start.6
  75.0 15.1 %copy-start.3 = (bf16[768,128]{1,0:T(8,128)(2,1)S(1)}, bf16[768,128]{1,0:T(8,128)(2,1)}, u32[]{:S(2)}) copy-start(bf16[768,128]{1,0:T(8,128)(2,1)} %fusion.1.unshift_ref) | copy-start | bytes 589828
  75.0 15.1 %copy-start.15 = (bf16[128,1024]{1,0:T(8,128)(2,1)S(1)}, bf16[128,1024]{1,0:T(8,128)(2,1)}, u32[]{:S(2)}) copy-start(bf16[128,1024]{1,0:T(8,128)(2,1)} %copy-done.14) | copy-start | bytes 786436
  75.0 15.1 %copy-start.17 = (bf16[128,1024]{1,0:T(8,128)(2,1)S(1)}, bf16[128,1024]{1,0:T(8,128)(2,1)}, u32[]{:S(2)}) copy-start(bf16[128,1024]{1,0:T(8,128)(2,1)} %copy-done.16) | copy-start | bytes 786436
  75.0 52.1 %collective-permute-start.3 = (bf16[128,1024]{1,0:T(8,128)(2,1)S(1)}, bf16[128,1024]{1,0:T(8,128)(2,1)S(1)}, u32[]{:S(2)}, u32[]{:S(2)}) collective-permute-start(bf16[128,1024]{1,0:T(8,128)(2,1)S(1)} %get-tuple-element.73), channel_id=1, source_target_pairs={{0,8},{8,16},{16,24},{24,32},{32,40},{40,48},{48,56},{56,64},{64,7... | collective-permute-start | bytes 786440 | tf_op jit(solution)/shard_map/ppermute | solution.py:31
  78.1 1.1 copy-start.5
  79.4 0.7 copy-start.18
  80.1 47.2 %collective-permute-start.4 = (bf16[128,1024]{1,0:T(8,128)(2,1)S(1)}, bf16[128,1024]{1,0:T(8,128)(2,1)S(1)}, u32[]{:S(2)}, u32[]{:S(2)}) collective-permute-start(bf16[128,1024]{1,0:T(8,128)(2,1)S(1)} %get-tuple-element.74), channel_id=1, source_target_pairs={{0,248},{8,0},{16,8},{24,16},{32,24},{40,32},{48,40},{56,48},{64,5... | collective-permute-start | bytes 786440 | tf_op jit(solution)/shard_map/ppermute | solution.py:31
  90.1 49.9 %collective-permute-start.1 = (bf16[128,1024]{1,0:T(8,128)(2,1)S(1)}, bf16[128,1024]{1,0:T(8,128)(2,1)S(1)}, u32[]{:S(2)}, u32[]{:S(2)}) collective-permute-start(bf16[128,1024]{1,0:T(8,128)(2,1)S(1)} %get-tuple-element.68), channel_id=1, source_target_pairs={{0,8},{8,16},{16,24},{24,32},{32,40},{40,48},{48,56},{56,64},{64,7... | collective-permute-start | bytes 786440 | tf_op jit(solution)/shard_map/ppermute | solution.py:31
  90.1 1.0 copy-start.19
  91.1 23.2 %copy-start.11 = (bf16[128,1024]{1,0:T(8,128)(2,1)S(1)}, bf16[128,1024]{1,0:T(8,128)(2,1)}, u32[]{:S(2)}) copy-start(bf16[128,1024]{1,0:T(8,128)(2,1)} %copy-done.10) | copy-start | bytes 786436
  91.1 23.2 %copy-start.13 = (bf16[128,1024]{1,0:T(8,128)(2,1)S(1)}, bf16[128,1024]{1,0:T(8,128)(2,1)}, u32[]{:S(2)}) copy-start(bf16[128,1024]{1,0:T(8,128)(2,1)} %copy-done.12) | copy-start | bytes 786436
  111.7 30.7 %collective-permute-start.2 = (bf16[128,1024]{1,0:T(8,128)(2,1)S(1)}, bf16[128,1024]{1,0:T(8,128)(2,1)S(1)}, u32[]{:S(2)}, u32[]{:S(2)}) collective-permute-start(bf16[128,1024]{1,0:T(8,128)(2,1)S(1)} %get-tuple-element.69), channel_id=1, source_target_pairs={{0,248},{8,0},{16,8},{24,16},{32,24},{40,32},{48,40},{56,48},{64,5... | collective-permute-start | bytes 786440 | tf_op jit(solution)/shard_map/ppermute | solution.py:31
  155.2 0.8 copy-start.2
  155.9 0.7 copy-start.4
  156.6 0.7 copy-start.9
  162.3 32.1 %all-to-all-start.1 = ((f32[256,4,128]{2,1,0:T(4,128)}), f32[256,4,128]{2,1,0:T(4,128)S(1)}, u32[]{:S(2)}, u32[]{:S(2)}) async-start(f32[256,4,128]{2,1,0:T(4,128)} %bitcast.20), calls=%async_computation.1 | async-start | bytes 1048576 | tf_op jit(solution)/shard_map/all_to_all | solution.py:367
  174.1 43.6 %collective-permute-start.9 = (bf16[16,12288]{1,0:T(8,128)(2,1)}, bf16[16,12288]{1,0:T(8,128)(2,1)S(1)}, u32[]{:S(2)}, u32[]{:S(2)}) collective-permute-start(bf16[16,12288]{1,0:T(8,128)(2,1)} %copy-done.9), channel_id=1, source_target_pairs={{0,248},{8,0},{16,8},{24,16},{32,24},{40,32},{48,40},{56,48},{64,5... | collective-permute-start | bytes 1179656 | tf_op jit(solution)/shard_map/ppermute | solution.py:31
  195.3 33.4 %all-to-all-start.2 = ((f32[32,4,128]{2,1,0:T(4,128)}), f32[32,4,128]{2,1,0:T(4,128)S(1)}, u32[]{:S(2)}, u32[]{:S(2)}) async-start(f32[32,4,128]{2,1,0:T(4,128)} %broadcast_in_dim.72), calls=%async_computation.2 | async-start | bytes 131072 | tf_op jit(solution)/shard_map/all_to_all | solution.py:369
  217.7 0.7 copy-start.22

commit v2 on v1

v2 whole, which is shorter than its diff:
```python
import functools

import jax
import jax.numpy as jnp
from jax import lax
from jax.experimental import pallas as pl
from jax.experimental.pallas import tpu as pltpu
from jax.sharding import PartitionSpec as P

C = 4096
GROUP = 16
LEN = 128
SHORT = 7
TOK = 128
TAIL = 16
WIDE = TOK + TAIL
LANES = 128
BLK = 512
SLABS = BLK // LANES
PER_SLAB = LANES // GROUP
BLOCKS = C // BLK
UNROLL = 4
CHUNKS = ((0, 2), (2, 2), (4, 2), (6, 2))
PACK = 32
FAR = 1 << 20
VMEM_LIMIT = 48 * 1024 * 1024

bf16 = jnp.bfloat16
f32 = jnp.float32


def ring(block, distance):
    count = lax.axis_size("ctx")
    return lax.ppermute(block, "ctx", [(i, (i + distance) % count) for i in range(count)])


def dot(a, b):
    return jnp.dot(a, b, preferred_element_type=f32)


def in_hbm(array):
    return pltpu.with_memory_space_constraint(array, pltpu.HBM)


def latest_start(listed, places):
    latest = jnp.full(places.shape, -FAR, jnp.int32)
    for k in range(listed.shape[1]):
        start = listed[:, k : k + 1]
        latest = jnp.maximum(latest, jnp.where((start < TOK) & (start <= places), start, -FAR))
    return latest


def put(ref, place, linked):
    ref[place] = jnp.where(linked, 1.0, 0.0).astype(ref.dtype)


def bounds(listed):
    usable = listed < TOK
    first = jnp.min(jnp.where(usable, listed, FAR), axis=1, keepdims=True)
    last = jnp.max(jnp.where(usable, listed, -FAR), axis=1, keepdims=True)
    return first, last


def shift_kernel(starts_ref, shift_ref, send_ref):
    listed = starts_ref[...]
    first, last = bounds(listed)
    here = lax.broadcasted_iota(jnp.int32, (TOK, WIDE), 0)
    cols = lax.broadcasted_iota(jnp.int32, (TOK, WIDE), 1)
    cols = jnp.where(cols < TOK, cols, jnp.where(cols < TOK + SHORT - 1, cols - (TOK + SHORT - 1), FAR))
    latest_here = latest_start(listed, here)
    for lag in range(1, SHORT):
        place = slice((lag - 1) * TOK, lag * TOK)
        put(shift_ref, place, (cols == here - lag) & (latest_here <= here - lag))
    side = lax.broadcasted_iota(jnp.int32, (TOK, 2), 1)
    rows = lax.broadcasted_iota(jnp.int32, (TOK, 2), 0)
    put(send_ref, slice(0, TOK), jnp.where(side == 0, rows - last, first - 1 - rows) >= 0)


def link_kernel(starts_ref, mask_ref, unshift_ref):
    listed = starts_ref[...]
    first, last = bounds(listed)
    t = lax.broadcasted_iota(jnp.int32, (TOK, TOK), 0)
    s = lax.broadcasted_iota(jnp.int32, (TOK, TOK), 1)
    back = TOK - 1 - t
    latest_t, latest_s = latest_start(listed, t), latest_start(listed, s)
    put(mask_ref, 0, (s <= t) & (latest_t <= s))
    put(mask_ref, 1, (s > t) & (t < first))
    put(mask_ref, 2, (t <= s) & (latest_s <= t))
    put(mask_ref, 3, (t > s) & (t >= last))
    put(mask_ref, 4, (s <= back) & (latest_start(listed, back) <= s))
    put(mask_ref, 5, (s > back) & (back < first))
    put(mask_ref, 6, s == back)
    put(mask_ref, 7, (s + t == TOK) | (s + t == 0))
    rows = lax.broadcasted_iota(jnp.int32, (TAIL, TOK), 0)
    tail = jnp.where(rows < SHORT - 1, rows - (SHORT - 1), FAR)
    later = lax.broadcasted_iota(jnp.int32, (TAIL, TOK), 1)
    latest_later = latest_start(listed, later)
    for lag in range(1, SHORT):
        first_row = (lag - 1) * WIDE
        put(unshift_ref, slice(first_row, first_row + TOK), (s == t + lag) & (latest_s <= t))
        linked = (later == tail + lag) & (latest_later <= tail)
        put(unshift_ref, slice(first_row + TOK, first_row + WIDE), linked)


def table_call(kernel, shapes, starts, name):
    return pl.pallas_call(
        kernel,
        in_specs=[pl.BlockSpec(memory_space=pltpu.VMEM)],
        out_specs=[pl.BlockSpec(memory_space=pltpu.VMEM)] * 2,
        out_shape=[jax.ShapeDtypeStruct(shape, dtype) for shape, dtype in shapes],
        cost_estimate=pl.CostEstimate(flops=5_000_000, bytes_accessed=1_000_000, transcendentals=0),
        name=name,
    )(starts)


def shift_call(starts):
    shapes = [(((SHORT - 1) * TOK, WIDE), bf16), ((TOK, 2), f32)]
    return table_call(shift_kernel, shapes, starts, "shifts")


def link_call(starts):
    shapes = [((8, TOK, TOK), bf16), (((SHORT - 1) * WIDE, TOK), bf16)]
    return table_call(link_kernel, shapes, starts, "links")


def short_sum(taps, near, moved, step):
    total = taps[0:1] * near
    for lag in range(1, SHORT):
        first = (lag - 1) * step
        total = total + taps[lag : lag + 1] * moved[first : first + TOK]
    return total


def tap_rows(packed):
    return jnp.concatenate([packed[0, 8 * k : 8 * k + 8] for k in range(SLABS)], axis=1)


def tail_rows(tail):
    tail = tail[...].astype(f32)
    empty = jnp.zeros((TAIL - tail.shape[0], tail.shape[1]), f32)
    return jnp.concatenate([tail, empty], axis=0).astype(bf16)


def feature_kernel(
    xq, xk, xv, tq, tk, tv, wq, wk, wv, grad_ref, shift_ref, send_ref,
    gate_send_ref, long_send_ref, feat_ref,
):
    feats = []
    for part, (x, tail, taps) in enumerate(((xq, tq, wq), (xk, tk, wk), (xv, tv, wv))):
        own = x[...]
        moved = dot(shift_ref[...], jnp.concatenate([own, tail_rows(tail)], axis=0))
        feats.append(short_sum(tap_rows(taps), own.astype(f32), moved, TOK))
        feat_ref[part] = feats[part]
    gate = (feats[1] * feats[2]).astype(bf16)
    long_in = (grad_ref[...].astype(f32) * feats[0]).astype(bf16)
    gate_send_ref[...] = (gate.astype(f32) * send_ref[:, 0:1]).astype(bf16)
    long_send_ref[...] = (long_in.astype(f32) * send_ref[:, 1:2]).astype(bf16)


def feature_call(chunk, proj, tail, params, grad_out, shifts, sends, per_shard):
    base, count = chunk
    wide = count * BLK

    def cols(part):
        return lambda j: (0, part * BLOCKS + base + j)

    def taps(part):
        def index(j):
            place = part * BLOCKS + base + j
            return (place // per_shard, place % per_shard, 0)

        return index

    whole = lambda j: (0, 0)
    here = pl.BlockSpec((TOK, BLK), lambda j: (0, j))
    return pl.pallas_call(
        feature_kernel,
        grid=(count,),
        in_specs=[pl.BlockSpec((TOK, BLK), cols(part)) for part in range(3)]
        + [pl.BlockSpec((SHORT - 1, BLK), cols(part)) for part in range(3)]
        + [pl.BlockSpec((1, PACK, LANES), taps(part)) for part in range(3)]
        + [
            pl.BlockSpec((TOK, BLK), cols(0)),
            pl.BlockSpec(shifts.shape, whole),
            pl.BlockSpec(sends.shape, whole),
        ],
        out_specs=[here, here, pl.BlockSpec((3, TOK, BLK), lambda j: (0, 0, j))],
        out_shape=[jax.ShapeDtypeStruct((TOK, wide), bf16)] * 2 + [pltpu.HBM((3, TOK, wide), f32)],
        compiler_params=pltpu.CompilerParams(vmem_limit_bytes=VMEM_LIMIT),
        cost_estimate=pl.CostEstimate(
            flops=2 * 3 * 768 * 144 * wide, bytes_accessed=12 * TOK * wide, transcendentals=0
        ),
        name="features",
    )(*[in_hbm(proj)] * 3, tail, tail, tail, params, params, params, in_hbm(grad_out), in_hbm(shifts), in_hbm(sends))


def main_kernel(
    gate_halo_ref, long_halo_ref, feat_ref, grad_ref, xq, xk, xv, tq, tk, tv, wq, wk, wv,
    skip_ref, filt_ref, mask_ref, unshift_ref, send_ref, *rest,
):
    (mixed_ref, source_ref, short_ref, lag_ref, skip_grad_ref, head_ref, end_ref,
     gate_ref, long_ref, long_out_ref, gate_grad_ref, feat_grad_ref, padded_ref,
     taps_ref, fore_ref, back_ref, ready_ref, sems) = rest[-18:]
    base = rest[0]
    count, step = pl.num_programs(0), pl.program_id(0)
    lane_group = lax.broadcasted_iota(jnp.int32, (TOK, LANES), 1) // GROUP

    def copies(at):
        slot = at % 2
        return [
            pltpu.make_async_copy(
                ready_ref.at[slot, part],
                source_ref.at[:, pl.ds(pl.multiple_of((part * BLOCKS + base + at) * BLK, BLK), BLK)],
                sems.at[slot, part],
            )
            for part in range(3)
        ]

    for part, (x, tail, taps) in enumerate(((xq, tq, wq), (xk, tk, wk), (xv, tv, wv))):
        padded_ref[part, :TOK] = x[...]
        padded_ref[part, TOK:] = tail_rows(tail)
        taps_ref[part] = tap_rows(taps)

    filt = filt_ref[0].astype(bf16)
    back_ref[...] = filt.astype(f32)
    fore_ref[...] = dot(filt, mask_ref[7])

    gate_ref[...] = (feat_ref[1] * feat_ref[2]).astype(bf16)
    long_ref[...] = (grad_ref[...].astype(f32) * feat_ref[0]).astype(bf16)

    def slab(at, carry):
        lanes = pl.ds(pl.multiple_of(at * LANES, LANES), LANES)
        own_long = long_ref[:, lanes]
        gates = jnp.concatenate([gate_ref[:, lanes], gate_halo_ref[:, lanes]], axis=0)
        longs = jnp.concatenate([own_long, long_halo_ref[:, lanes]], axis=0)
        turned = dot(mask_ref[6], own_long).astype(bf16)
        rows = pl.ds(pl.multiple_of(at * PER_SLAB, PER_SLAB), PER_SLAB)
        fore = fore_ref[rows, :]
        back = back_ref[rows, :]
        own_mask = mask_ref[4].astype(f32)
        before_mask = mask_ref[5].astype(f32)
        def bands(rows_of, first, second):
            made = []
            for g in range(PER_SLAB):
                band = jnp.broadcast_to(rows_of[g : g + 1], (TOK, LANES))
                band = pltpu.roll(band, 0, 1, stride=1, stride_axis=0).astype(bf16)
                made.append(jnp.concatenate([band * first, band * second], axis=1))
            return jnp.concatenate(made, axis=0)

        def gathered(wide):
            total = wide[:TOK]
            for g in range(1, PER_SLAB):
                total = jnp.where(lane_group == g, wide[g * TOK : (g + 1) * TOK], total)
            return total

        out = gathered(dot(bands(fore, mask_ref[0], mask_ref[1]), gates))
        spread = gathered(dot(bands(back, mask_ref[2], mask_ref[3]), longs))
        picked = jnp.concatenate(
            [jnp.where(lane_group == g, turned, jnp.zeros_like(turned)) for g in range(PER_SLAB)], axis=0
        )
        product = lax.dot_general(picked, gates, (((1,), (1,)), ((), ())), preferred_element_type=f32)
        sums = []
        for g in range(PER_SLAB):
            place = slice(g * TOK, (g + 1) * TOK)
            kept = product[place, :TOK] * own_mask + product[place, TOK:] * before_mask
            kept = pltpu.roll(kept, 0, 1, stride=1, stride_axis=0)
            sums.append(jnp.sum(kept, axis=0, keepdims=True))
        long_out_ref[:, lanes] = out
        gate_grad_ref[:, lanes] = spread
        lag_ref[rows, :] = jnp.concatenate(sums, axis=0)
        return carry

    lax.fori_loop(0, SLABS, slab, 0, unroll=UNROLL)
    gate = gate_ref[...].astype(f32)
    upstream = grad_ref[...].astype(f32)
    query = feat_ref[0]
    skip = tap_rows(skip_ref)[7:8]
    combined = long_out_ref[...] + skip * gate
    through = upstream * query
    mixed_ref[...] = (query * combined).astype(bf16)
    feat_grad_ref[0] = upstream * combined
    gate_grad = gate_grad_ref[...] + skip * through
    feat_grad_ref[1] = gate_grad * feat_ref[2]
    feat_grad_ref[2] = gate_grad * feat_ref[1]
    skip_grad = jnp.sum(through * gate, axis=0, keepdims=True)
    for k in range(SLABS):
        skip_grad_ref[k] = skip_grad[:, k * LANES : (k + 1) * LANES]

    @pl.when(step >= 2)
    def _():
        for copy in copies(step - 2):
            copy.wait()

    def column_part(part, carry):
        feat_grad = feat_grad_ref[part]
        moved = dot(unshift_ref[...], feat_grad.astype(bf16))
        near = padded_ref[part, :TOK].astype(f32)
        tail = padded_ref[part, TOK:].astype(f32)
        sums = [jnp.sum(near * feat_grad, axis=0, keepdims=True)]
        for lag in range(1, SHORT):
            first = (lag - 1) * WIDE
            own = jnp.sum(near * moved[first : first + TOK], axis=0, keepdims=True)
            before = jnp.sum(tail * moved[first + TOK : first + WIDE], axis=0, keepdims=True)
            sums.append(own + before)
        sums.append(jnp.zeros_like(sums[0]))
        sums = jnp.concatenate(sums, axis=0)
        for k in range(SLABS):
            short_ref[part, k] = sums[:, k * LANES : (k + 1) * LANES]
        source = short_sum(taps_ref[part], feat_grad, moved, WIDE)
        ready_ref[step % 2, part] = source.astype(bf16)
        end_ref[part] = source[TOK - 8 :]
        head_ref[part] = (feat_grad[:TAIL] * send_ref[:TAIL, 1:2]).astype(bf16)
        return carry

    lax.fori_loop(0, 3, column_part, 0)
    for copy in copies(step):
        copy.start()

    @pl.when(step == count - 1)
    def _():
        @pl.when(count >= 2)
        def _():
            for copy in copies(step - 1):
                copy.wait()

        for copy in copies(step):
            copy.wait()


def main_call(chunk, gate_halo, long_halo, feats, grad_out, proj, tail, params,
              masks, unshifts, sends, per_shard, kept):
    base, count = chunk
    shards = params.shape[0]
    own_blocks = BLOCKS // shards
    local = pl.BlockSpec((TOK, BLK), lambda j: (0, j))
    first_cols = pl.BlockSpec((TOK, BLK), lambda j: (0, base + j))

    def cols(rows, part):
        return pl.BlockSpec((rows, BLK), lambda j: (0, part * BLOCKS + base + j))

    def taps(part):
        def index(j):
            place = part * BLOCKS + base + j
            return (place // per_shard, place % per_shard, 0)

        return pl.BlockSpec((1, PACK, LANES), index)

    def skips(j):
        return ((base + j) // own_blocks, (base + j) % own_blocks, 0)

    def filters(j):
        return ((base + j) // own_blocks, per_shard + (base + j) % own_blocks, 0)

    def whole(array):
        return pl.BlockSpec(array.shape, lambda j: (0,) * array.ndim)

    groups = BLK // GROUP
    operands = [gate_halo, long_halo, feats, in_hbm(grad_out), *[in_hbm(proj)] * 3, tail, tail, tail,
                params, params, params, params, params, *[in_hbm(table) for table in (masks, unshifts, sends)]]
    in_specs = (
        [local, local, pl.BlockSpec((3, TOK, BLK), lambda j: (0, 0, j)), first_cols]
        + [cols(TOK, part) for part in range(3)]
        + [cols(SHORT - 1, part) for part in range(3)]
        + [taps(part) for part in range(3)]
        + [pl.BlockSpec((1, PACK, LANES), skips), pl.BlockSpec((1, PACK, LANES), filters)]
        + [whole(masks), whole(unshifts), whole(sends)]
    )
    aliases = {}
    if kept is not None:
        aliases = {len(operands) + k: k for k in range(len(kept))}
        operands = operands + list(kept)
        in_specs = in_specs + [pl.BlockSpec(memory_space=pl.ANY)] * len(kept)
    slabs = C // LANES
    places = len(operands) - (0 if kept is None else len(kept))

    def kernel(*refs):
        main_kernel(*refs[:places], base, *refs[places:])

    return pl.pallas_call(
        kernel,
        grid=(count,),
        in_specs=in_specs,
        out_specs=[
            first_cols,
            pl.BlockSpec(memory_space=pl.ANY),
            pl.BlockSpec((3, SLABS, 8, LANES), lambda j: (0, base + j, 0, 0)),
            pl.BlockSpec((groups, LANES), lambda j: (base + j, 0)),
            pl.BlockSpec((SLABS, 1, LANES), lambda j: (base + j, 0, 0)),
            pl.BlockSpec((3, TAIL, BLK), lambda j: (0, 0, base + j)),
            pl.BlockSpec((3, 8, BLK), lambda j: (0, 0, base + j)),
        ],
        out_shape=[
            jax.ShapeDtypeStruct((TOK, C), bf16),
            jax.ShapeDtypeStruct((TOK, 3 * C), bf16),
            jax.ShapeDtypeStruct((3, slabs, 8, LANES), f32),
            jax.ShapeDtypeStruct((C // GROUP, LANES), f32),
            jax.ShapeDtypeStruct((slabs, 1, LANES), f32),
            jax.ShapeDtypeStruct((3, TAIL, C), bf16),
            jax.ShapeDtypeStruct((3, 8, C), f32),
        ],
        scratch_shapes=[
            pltpu.VMEM((TOK, BLK), bf16),
            pltpu.VMEM((TOK, BLK), bf16),
            pltpu.VMEM((TOK, BLK), f32),
            pltpu.VMEM((TOK, BLK), f32),
            pltpu.VMEM((3, TOK, BLK), f32),
            pltpu.VMEM((3, TOK + TAIL, BLK), bf16),
            pltpu.VMEM((3, 8, BLK), f32),
            pltpu.VMEM((PACK, LANES), f32),
            pltpu.VMEM((PACK, LANES), f32),
            pltpu.VMEM((2, 3, TOK, BLK), bf16),
            pltpu.SemaphoreType.DMA((2, 3)),
        ],
        input_output_aliases=aliases,
        compiler_params=pltpu.CompilerParams(vmem_limit_bytes=VMEM_LIMIT),
        cost_estimate=pl.CostEstimate(
            flops=5_000_000_000 * count, bytes_accessed=40 * TOK * count * BLK, transcendentals=0
        ),
        name="main",
    )(*operands)


def patch_kernel(starts_ref, source_ref, end_ref, head_ref, params_ref, out_ref):
    rows = lax.broadcasted_iota(jnp.int32, (8, BLK), 0) + (TOK - 8)
    listed = starts_ref[...]
    last = jnp.max(jnp.where(listed < TOK, listed, -FAR), axis=1, keepdims=True)
    keep = jnp.where(rows >= last, 1.0, 0.0)
    shards = params_ref.shape[0]
    per_shard = 3 * BLOCKS // shards
    for place in range(3 * BLOCKS):
        part, first = place // BLOCKS, place % BLOCKS * BLK
        own = slice(first, first + BLK)
        head = head_ref[part, :, own].astype(f32)
        ahead = jnp.concatenate([jnp.zeros_like(head), head], axis=0)
        first = place % per_shard * PACK
        taps = tap_rows(params_ref[pl.ds(place // per_shard, 1), first : first + PACK])
        extra = jnp.zeros_like(head)
        for lag in range(1, SHORT):
            extra = extra + taps[lag : lag + 1] * ahead[lag : lag + 8]
        final = end_ref[part, :, own] + extra * keep
        lanes = slice(place * BLK, (place + 1) * BLK)
        before = source_ref[:, lanes].astype(f32)[:8]
        out_ref[:, lanes] = jnp.concatenate([before, final], axis=0).astype(bf16)


def patch_call(starts, source, end, head, params):
    rows = TOK // TAIL - 1

    def whole(array):
        return pl.BlockSpec(array.shape, lambda j: (0,) * array.ndim)

    strip = pl.BlockSpec((TAIL, 3 * C), lambda j: (rows, 0))
    return pl.pallas_call(
        patch_kernel,
        grid=(1,),
        in_specs=[whole(starts), strip, whole(end), whole(head), whole(params)],
        out_specs=strip,
        out_shape=jax.ShapeDtypeStruct(source.shape, bf16),
        input_output_aliases={1: 0},
        compiler_params=pltpu.CompilerParams(vmem_limit_bytes=VMEM_LIMIT),
        cost_estimate=pl.CostEstimate(flops=1_000_000, bytes_accessed=2_000_000, transcendentals=0),
        name="patch",
    )(starts, source, end, head, params)


def prepare_kernel(starts_hbm, source_hbm, taps_hbm, skip_hbm, filt_hbm, tail_ref, packed_ref,
                   starts_ref, source_ref, taps_ref, skip_ref, filt_ref, sems):
    copies = [
        pltpu.make_async_copy(starts_hbm, starts_ref, sems.at[0]),
        pltpu.make_async_copy(source_hbm.at[pl.ds(TOK - TAIL, TAIL), :], source_ref, sems.at[1]),
        pltpu.make_async_copy(taps_hbm, taps_ref, sems.at[2]),
        pltpu.make_async_copy(skip_hbm, skip_ref, sems.at[3]),
        pltpu.make_async_copy(filt_hbm, filt_ref, sems.at[4]),
    ]
    for copy in copies:
        copy.start()
    for copy in copies:
        copy.wait()
    listed = starts_ref[...]
    last = jnp.max(jnp.where(listed < TOK, listed, -FAR), axis=1, keepdims=True)
    rows = lax.broadcasted_iota(jnp.int32, (SHORT - 1, 1), 0) + (TOK - SHORT + 1)
    tail = source_ref[...].astype(f32)[TAIL - SHORT + 1 :]
    tail_ref[...] = (tail * jnp.where(rows >= last, 1.0, 0.0)).astype(bf16)
    own, slabs = skip_ref.shape[1], taps_ref.shape[1] // LANES
    empty = jnp.zeros((1, LANES), f32)
    rows = []
    for k in range(slabs):
        lanes = slice(k * LANES, (k + 1) * LANES)
        rows += [taps_ref[:, lanes], skip_ref[:, lanes] if k * LANES < own else empty]
    packed = jnp.concatenate(rows + [filt_ref[...]], axis=0)
    packed_ref[...] = packed


def prepare_call(starts, source, short_taps, skip, filt, shards):
    own = skip.shape[0]
    rows = short_taps.shape[1] // LANES * 8 + filt.shape[0]
    return pl.pallas_call(
        prepare_kernel,
        in_specs=[pl.BlockSpec(memory_space=pltpu.HBM)] * 5,
        out_specs=[pl.BlockSpec(memory_space=pltpu.VMEM)] * 2,
        out_shape=[
            jax.ShapeDtypeStruct((SHORT - 1, 3 * C), bf16),
            jax.ShapeDtypeStruct((rows, LANES), f32),
        ],
        scratch_shapes=[
            pltpu.VMEM(starts.shape, jnp.int32),
            pltpu.VMEM((TAIL, 3 * C), bf16),
            pltpu.VMEM(short_taps.shape, f32),
            pltpu.VMEM((1, own), f32),
            pltpu.VMEM(filt.shape, f32),
            pltpu.SemaphoreType.DMA((5,)),
        ],
        compiler_params=pltpu.CompilerParams(vmem_limit_bytes=VMEM_LIMIT),
        cost_estimate=pl.CostEstimate(flops=1_000_000, bytes_accessed=2_000_000, transcendentals=0),
        name="prepare",
    )(*[in_hbm(array) for array in (starts, source, short_taps, skip[None], filt)])


def body(proj, short_taps, long_filter, skip, grad_out, starts):
    shards, count = lax.axis_size("fsdp"), lax.axis_size("ctx")
    source, upstream = proj[0], grad_out[0]
    shifts, sends = shift_call(starts[0])
    masks, unshifts = link_call(starts[0])
    wide = short_taps.shape[1]
    per_shard = wide // BLK
    tail, packed = prepare_call(starts[0], source, short_taps, skip, long_filter.T, shards)
    tail = ring(tail, 1)
    params = lax.all_gather(packed, "fsdp", axis=0)
    parts = []
    for chunk in CHUNKS:
        gate_send, long_send, feats = feature_call(
            chunk, source, tail, params, upstream, shifts, sends, per_shard
        )
        parts.append((ring(gate_send, 1), ring(long_send, -1), feats))
    kept = None
    for chunk, part in zip(CHUNKS, parts):
        kept = main_call(
            chunk, *part, upstream, source, tail, params, masks, unshifts,
            sends, per_shard, kept,
        )
    mixed, grad_source, short_sums, lag_sums, skip_sums, head, end = kept
    head = ring(head[:, :8], -1)

    skip_slabs = C // LANES // shards
    skip_sums = skip_sums.reshape(shards, skip_slabs, 1, LANES)
    short_sums = short_sums.reshape(shards, -1, 8, LANES)
    room = ((0, 0), (0, short_sums.shape[1] - skip_slabs), (7, 0), (0, 0))
    short_sums = short_sums + jnp.pad(skip_sums, room)
    sums = jnp.concatenate(
        [short_sums.reshape(shards, -1, LANES), lag_sums.reshape(shards, -1, LANES)], axis=1
    )
    piece = sums.shape[1] // count
    sums = sums.reshape(shards * count, piece, LANES)
    sums = jnp.sum(lax.all_to_all(sums, ("fsdp", "ctx"), 0, 0, tiled=True), axis=0)
    sums = sums * (float(shards * count * TOK) ** -0.5)
    grad_source = patch_call(starts[0], grad_source, end, head, params)
    sums = lax.all_to_all(
        jnp.broadcast_to(sums[None], (count,) + sums.shape), "ctx", 0, 0, tiled=True
    ).reshape(count * piece, LANES)
    slabs = 3 * C // LANES // shards
    grad_short = sums[: slabs * 8].reshape(slabs, 8, LANES)
    grad_skip = grad_short[:skip_slabs, 7].reshape(-1)
    grad_short = grad_short[:, :SHORT].transpose(1, 0, 2).reshape(SHORT, -1)
    grad_long = sums[slabs * 8 :, ::-1].T
    return mixed[None], grad_source[None], grad_short, grad_long, grad_skip


def solution(mesh):
    placed = (
        P("fsdp", "ctx", None),
        P(None, "fsdp"),
        P(None, "fsdp"),
        P("fsdp"),
        P("fsdp", "ctx", None),
        P("fsdp", "ctx", None),
    )
    return jax.shard_map(
        body,
        mesh=mesh,
        in_specs=placed,
        out_specs=(
            P("fsdp", "ctx", None),
            P("fsdp", "ctx", None),
            P(None, "fsdp"),
            P(None, "fsdp"),
            P("fsdp"),
        ),
        check_vma=False,
    )
```

time: 232 us -> 200 us (0.86)
  local copies, waits for them, and re-layouts: 23.1 us -> 2.56 us
  blocking collectives: 0 us -> 17.7 us
  other arithmetic: 13.7 us -> 1.17 us
  waiting for transfers between devices: 36.8 us -> 25.4 us
  Pallas kernels: 69.2 us -> 62.7 us
    all_gather x0 -> x1, blocking collectives: none -> 17.7 us  [body(): params = lax.all_gather(packed, 'fsdp', axis=0)]
    unnamed x54 -> x10, local copies, waits for them, and re-layouts: 12.9 us -> 0.02 us
    all_to_all x1 -> x0, waiting for transfers between devices: 11.2 us -> none  [body(): lax.all_to_all(jnp.broadcast_to(packed[None], (shards,) + packed.shape),...]
    pallas_call x5 -> x8, Pallas kernels: 56.4 us -> 46.7 us  [the longest x4 39.6 us: main_call(): pl.pallas_call(kernel, grid=(count,), in_specs=in_specs, out_specs=[first...]
    all_to_all x1, starting transfers between devices: 21.1 us -> 12.7 us  [body(): lax.all_to_all(jnp.broadcast_to(sums[None], (count,) + sums.shape), 'ctx'...]
    ppermute x10, starting transfers between devices: 49.5 us -> 57.1 us  [ring(): lax.ppermute(block, 'ctx', [(i, (i + distance) % count) for i in range(co...]
    all_to_all x1, starting transfers between devices: 11.7 us -> 19.3 us  [body(): lax.all_to_all(sums, ('fsdp', 'ctx'), 0, 0, tiled=True)]
    ppermute x10, waiting for transfers between devices: 10.3 us -> 5.32 us  [ring(): lax.ppermute(block, 'ctx', [(i, (i + distance) % count) for i in range(co...]
  transfers between devices with their start and end apart: 13 -> 12, of which waited for: 6 -> 3; matrix products, arithmetic and copies ran while one was open for 6% -> 0% of each run, Pallas kernels for 23% -> 24%
where the time goes in v2:
time: 200 us; the launch traced here: 199 us
  starting transfers between devices  89 us (44%)
  Pallas kernels  62.7 us (31%)
  waiting for transfers between devices  25.4 us (13%)
  blocking collectives  17.7 us (9%)
  local copies, waits for them, and re-layouts  2.56 us (1%)
    ppermute x10, starting transfers between devices, ring(): lax.ppermute(block, 'ctx', [(i, (i + distance) % count) for i in range(co...  57.1 us
    pallas_call x4, Pallas kernels, main_call(): pl.pallas_call(kernel, grid=(count,), in_specs=in_specs, out_specs=[first...  39.6 us
    all_to_all x1, starting transfers between devices, body(): lax.all_to_all(sums, ('fsdp', 'ctx'), 0, 0, tiled=True)  19.3 us
    all_gather x1, blocking collectives, body(): params = lax.all_gather(packed, 'fsdp', axis=0)  17.7 us
    pallas_call x4, Pallas kernels, feature_call(): pl.pallas_call(feature_kernel, grid=(count,), in_specs=[pl.BlockSpec((TOK...  16 us
    all_to_all x1, starting transfers between devices, body(): lax.all_to_all(jnp.broadcast_to(sums[None], (count,) + sums.shape), 'ctx'...  12.7 us
    all_to_all x1, waiting for transfers between devices, body(): lax.all_to_all(sums, ('fsdp', 'ctx'), 0, 0, tiled=True)  10.2 us
    all_to_all x1, waiting for transfers between devices, body(): lax.all_to_all(jnp.broadcast_to(sums[None], (count,) + sums.shape), 'ctx'...  9.86 us
  transfers between devices with their start and end apart: 12, of which 3 were waited for; matrix products, arithmetic and copies ran while one was open for 0% of the time, Pallas kernels for 24%

profile of v2, /device:TPU:32, one launch (start us, length us, event | category | flops | bytes accessed | tf_op | source)
XLA Modules:
  0.0 199.3 jit_solution(3904699484386297446)
XLA Ops:
  0.6 1.3 prepare.1
  1.9 6.4 %collective-permute-start = (bf16[6,12288]{1,0:T(8,128)(2,1)S(1)}, bf16[6,12288]{1,0:T(8,128)(2,1)S(1)}, u32[]{:S(2)}, u32[]{:S(2)}) collective-permute-start(bf16[6,12288]{1,0:T(8,128)(2,1)S(1)} %get-tuple-element.51), channel_id=1, source_target_pairs={{0,8},{8,16},{16,24},{24,32},{32,40},{40,48},{48,56},{56,64},{64,7... | collective-permute-start | bytes 442376 | tf_op jit(solution)/shard_map/ppermute | solution.py:34
  8.3 1.7 shifts.1
  9.9 17.7 %all-gather = f32[1024,128]{1,0:T(8,128)S(1)} all-gather(f32[128,128]{1,0:T(8,128)S(1)} %get-tuple-element.52), channel_id=2, replica_groups=mesh['ctx'=32,'fsdp'=8] {'fsdp'}, dimensions={0}, use_global_device_ids=true | all-gather | bytes 589824 | tf_op jit(solution)/shard_map/all_gather | solution.py:528
  27.6 0.0 collective-permute-done.tq.tk.tv.refs_7_.refs_8_.refs_9_
  27.6 3.9 %features.7 = (bf16[128,1024]{1,0:T(8,128)(2,1)S(1)}, bf16[128,1024]{1,0:T(8,128)(2,1)S(1)}, f32[3,128,1024]{2,1,0:T(8,128)}) custom-call(bf16[128,12288]{1,0:T(8,128)(2,1)} %bitcast.65, bf16[128,12288]{1,0:T(8,128)(2,1)} %bitcast.66, bf16[128,12288]{1,0:T(8,128)(2,1)} %bitcast.67, ...), custom_call_target="tpu_custom_call" | custom-call | flops 679477248 | bytes 1572864 | tf_op jit(solution)/shard_map/features/pallas_call | solution.py:176
  31.6 0.8 collective-permute-start.7
  32.4 9.3 %collective-permute-start.8 = (bf16[128,1024]{1,0:T(8,128)(2,1)S(1)}, bf16[128,1024]{1,0:T(8,128)(2,1)S(1)}, u32[]{:S(2)}, u32[]{:S(2)}) collective-permute-start(bf16[128,1024]{1,0:T(8,128)(2,1)S(1)} %get-tuple-element.67), channel_id=1, source_target_pairs={{0,248},{8,0},{16,8},{24,16},{32,24},{40,32},{48,40},{56,48},{64,5... | collective-permute-start | bytes 786440 | tf_op jit(solution)/shard_map/ppermute | solution.py:34
  41.7 1.8 links.1
  43.5 4.0 %features.6 = (bf16[128,1024]{1,0:T(8,128)(2,1)S(1)}, bf16[128,1024]{1,0:T(8,128)(2,1)S(1)}, f32[3,128,1024]{2,1,0:T(8,128)}) custom-call(bf16[128,12288]{1,0:T(8,128)(2,1)} %bitcast.68, bf16[128,12288]{1,0:T(8,128)(2,1)} %bitcast.69, bf16[128,12288]{1,0:T(8,128)(2,1)} %bitcast.70, ...), custom_call_target="tpu_custom_call" | custom-call | flops 679477248 | bytes 1572864 | tf_op jit(solution)/shard_map/features/pallas_call | solution.py:176
  47.5 0.0 collective-permute-start.5
  47.5 10.1 %collective-permute-start.6 = (bf16[128,1024]{1,0:T(8,128)(2,1)S(1)}, bf16[128,1024]{1,0:T(8,128)(2,1)S(1)}, u32[]{:S(2)}, u32[]{:S(2)}) collective-permute-start(bf16[128,1024]{1,0:T(8,128)(2,1)S(1)} %get-tuple-element.64), channel_id=1, source_target_pairs={{0,248},{8,0},{16,8},{24,16},{32,24},{40,32},{48,40},{56,48},{64,5... | collective-permute-start | bytes 786440 | tf_op jit(solution)/shard_map/ppermute | solution.py:34
  57.6 4.0 %features.5 = (bf16[128,1024]{1,0:T(8,128)(2,1)S(1)}, bf16[128,1024]{1,0:T(8,128)(2,1)S(1)}, f32[3,128,1024]{2,1,0:T(8,128)}) custom-call(bf16[128,12288]{1,0:T(8,128)(2,1)} %bitcast.71, bf16[128,12288]{1,0:T(8,128)(2,1)} %bitcast.72, bf16[128,12288]{1,0:T(8,128)(2,1)} %bitcast.73, ...), custom_call_target="tpu_custom_call" | custom-call | flops 679477248 | bytes 1572864 | tf_op jit(solution)/shard_map/features/pallas_call | solution.py:176
  61.6 0.0 copy-start.4
  61.6 0.0 collective-permute-start.3
  61.6 4.1 %features.4 = (bf16[128,1024]{1,0:T(8,128)(2,1)S(1)}, bf16[128,1024]{1,0:T(8,128)(2,1)S(1)}, f32[3,128,1024]{2,1,0:T(8,128)}) custom-call(bf16[128,12288]{1,0:T(8,128)(2,1)} %bitcast.76, bf16[128,12288]{1,0:T(8,128)(2,1)} %bitcast.75, bf16[128,12288]{1,0:T(8,128)(2,1)} %bitcast.74, ...), custom_call_target="tpu_custom_call" | custom-call | flops 679477248 | bytes 1572864 | tf_op jit(solution)/shard_map/features/pallas_call | solution.py:176
  65.7 0.0 collective-permute-done.7.refs_0_
  65.7 10.1 %collective-permute-start.4 = (bf16[128,1024]{1,0:T(8,128)(2,1)S(1)}, bf16[128,1024]{1,0:T(8,128)(2,1)S(1)}, u32[]{:S(2)}, u32[]{:S(2)}) collective-permute-start(bf16[128,1024]{1,0:T(8,128)(2,1)S(1)} %get-tuple-element.61), channel_id=1, source_target_pairs={{0,248},{8,0},{16,8},{24,16},{32,24},{40,32},{48,40},{56,48},{64,5... | collective-permute-start | bytes 786440 | tf_op jit(solution)/shard_map/ppermute | solution.py:34
  75.8 0.0 collective-permute-done.8.refs_1_
  75.8 0.0 collective-permute-start.1
  75.8 0.0 copy-done.4
  75.8 0.0 copy-start.3
  75.8 9.9 %main.4 = (bf16[128,4096]{1,0:T(8,128)(2,1)}, bf16[128,12288]{1,0:T(8,128)(2,1)}, f32[3,32,8,128]{3,2,1,0:T(8,128)S(1)}, f32[256,128]{1,0:T(8,128)S(1)}, f32[32,...) custom-call(bf16[128,1024]{1,0:T(8,128)(2,1)S(1)} %collective-permute-done.7.refs_0_, ...), custom_call_target="tpu_custom_call" | custom-call | flops 10000000000 | bytes 5242880 | tf_op jit(solution)/shard_map/main/pallas_call | solution.py:379
  85.7 0.0 collective-permute-done.5.refs_0_
  85.7 10.2 %collective-permute-start.2 = (bf16[128,1024]{1,0:T(8,128)(2,1)S(1)}, bf16[128,1024]{1,0:T(8,128)(2,1)S(1)}, u32[]{:S(2)}, u32[]{:S(2)}) collective-permute-start(bf16[128,1024]{1,0:T(8,128)(2,1)S(1)} %get-tuple-element.56), channel_id=1, source_target_pairs={{0,248},{8,0},{16,8},{24,16},{32,24},{40,32},{48,40},{56,48},{64,5... | collective-permute-start | bytes 786440 | tf_op jit(solution)/shard_map/ppermute | solution.py:34
  95.9 0.0 collective-permute-done.6.refs_1_
  95.9 0.0 copy-done.3
  95.9 0.0 copy-start.2
  96.0 9.9 %main.5 = (bf16[128,4096]{1,0:T(8,128)(2,1)}, bf16[128,12288]{1,0:T(8,128)(2,1)}, f32[3,32,8,128]{3,2,1,0:T(8,128)S(1)}, f32[256,128]{1,0:T(8,128)S(1)}, f32[32,...) custom-call(bf16[128,1024]{1,0:T(8,128)(2,1)S(1)} %collective-permut, ...), custom_call_target="tpu_custom_call", output_to_operand_aliasing={{0}: (18, {}), {1}: (19, {}), {2}: (20, {}), {3}: (21, {}),... | custom-call | flops 10000000000 | bytes 5242880 | tf_op jit(solution)/shard_map/main/pallas_call | solution.py:379
  105.9 0.0 collective-permute-done.3.refs_0_
  105.9 0.0 collective-permute-done.4.refs_1_
  105.9 0.0 copy-done.2
  105.9 0.0 copy-start.1
  105.9 9.9 %main.6 = (bf16[128,4096]{1,0:T(8,128)(2,1)}, bf16[128,12288]{1,0:T(8,128)(2,1)}, f32[3,32,8,128]{3,2,1,0:T(8,128)S(1)}, f32[256,128]{1,0:T(8,128)S(1)}, f32[32,...) custom-call(bf16[128,1024]{1,0:T(8,128)(2,1)S(1)} %collective-permut, ...), custom_call_target="tpu_custom_call", output_to_operand_aliasing={{0}: (18, {}), {1}: (19, {}), {2}: (20, {}), {3}: (21, {}),... | custom-call | flops 10000000000 | bytes 5242880 | tf_op jit(solution)/shard_map/main/pallas_call | solution.py:379
  115.9 0.0 collective-permute-done.1.refs_0_
  115.9 5.3 %collective-permute-done.2.refs_1_ = bf16[128,1024]{1,0:T(8,128)(2,1)S(1)} collective-permute-done((bf16[128,1024]{1,0:T(8,128)(2,1)S(1)}, bf16[128,1024]{1,0:T(8,128)(2,1)S(1)}, u32[]{:S(2)}, u32[]{:S(2)}) %collective-permute-start.2) | collective-permute-done | bytes 262176 | tf_op jit(solution)/shard_map/ppermute | solution.py:34
  121.2 0.0 copy-done.1
  121.2 9.8 %main.7 = (bf16[128,4096]{1,0:T(8,128)(2,1)}, bf16[128,12288]{1,0:T(8,128)(2,1)}, f32[3,32,8,128]{3,2,1,0:T(8,128)S(1)}, f32[256,128]{1,0:T(8,128)S(1)}, f32[32,...) custom-call(bf16[128,1024]{1,0:T(8,128)(2,1)S(1)} %collective-permut, ...), custom_call_target="tpu_custom_call", output_to_operand_aliasing={{0}: (18, {}), {1}: (19, {}), {2}: (20, {}), {3}: (21, {}),... | custom-call | flops 10000000000 | bytes 5242880 | tf_op jit(solution)/shard_map/main/pallas_call | solution.py:379
  131.0 0.0 copy-start
  131.1 0.8 pad_maximum_fusion
  131.9 19.3 %all-to-all-start = ((f32[256,4,128]{2,1,0:T(4,128)}), f32[256,4,128]{2,1,0:T(4,128)S(1)}, u32[]{:S(2)}, u32[]{:S(2)}) async-start(f32[256,4,128]{2,1,0:T(4,128)} %bitcast.13), calls=%async_computation | async-start | bytes 1048576 | tf_op jit(solution)/shard_map/all_to_all | solution.py:554
  151.2 10.1 %collective-permute-start.9 = (bf16[3,8,4096]{2,1,0:T(8,128)(2,1)S(1)}, bf16[3,8,4096]{2,1,0:T(8,128)(2,1)S(1)}, u32[]{:S(2)}, u32[]{:S(2)}) collective-permute-start(bf16[3,8,4096]{2,1,0:T(8,128)(2,1)S(1)} %slice.19), channel_id=1, source_target_pairs={{0,248},{8,0},{16,8},{24,16},{32,24},{40,32},{48,40},{56,48},{64,5... | collective-permute-start | bytes 589832 | tf_op jit(solution)/shard_map/ppermute | solution.py:34
  161.3 10.2 %all-to-all-done = f32[256,4,128]{2,1,0:T(4,128)S(1)} async-done(((f32[256,4,128]{2,1,0:T(4,128)}), f32[256,4,128]{2,1,0:T(4,128)S(1)}, u32[]{:S(2)}, u32[]{:S(2)}) %all-to-all-start) | async-done | bytes 524320 | tf_op jit(solution)/shard_map/all_to_all | solution.py:554
  171.5 0.3 reduce_sum.9
  171.8 0.6 broadcast_in_dim.18
  172.4 12.7 %all-to-all-start.1 = ((f32[32,4,128]{2,1,0:T(4,128)}), f32[32,4,128]{2,1,0:T(4,128)S(1)}, u32[]{:S(2)}, u32[]{:S(2)}) async-start(f32[32,4,128]{2,1,0:T(4,128)} %broadcast_in_dim.18), calls=%async_computation.1 | async-start | bytes 131072 | tf_op jit(solution)/shard_map/all_to_all | solution.py:557
  185.1 0.0 collective-permute-done.9.head_ref
  185.1 0.0 copy-done
  185.1 2.4 %patch.1 = bf16[128,12288]{1,0:T(8,128)(2,1)} custom-call(s32[1,4]{1,0:T(1,128)S(1)} %bitcast.63, bf16[128,12288]{1,0:T(8,128)(2,1)} %get-tuple-element.91.source_ref, f32[3,8,4096]{2,1,0:T(8,128)S(1)} %get-tuple-element.92.end_ref, bf16[3,8,4096]{2,1,0:T(8,128)(2,1)S(1)} %collective-permute-done.9.head_ref, ...), custom_call_target="tpu_custom_call", output_to_operand_aliasing={{}: (1, {})} | custom-call | flops 1000000 | bytes 2000000 | tf_op jit(solution)/shard_map/patch/pallas_call | solution.py:453
  187.5 9.9 %all-to-all-done.1 = f32[32,4,128]{2,1,0:T(4,128)S(1)} async-done(((f32[32,4,128]{2,1,0:T(4,128)}), f32[32,4,128]{2,1,0:T(4,128)S(1)}, u32[]{:S(2)}, u32[]{:S(2)}) %all-to-all-start.1) | async-done | bytes 65568 | tf_op jit(solution)/shard_map/all_to_all | solution.py:557
  197.4 0.6 slice_bitcast_fusion
  198.0 0.6 slice.28
  198.6 0.7 rev.3
  (5 shorter events, 0.1 us)
Async XLA Ops:
  1.9 25.7 %collective-permute-start = (bf16[6,12288]{1,0:T(8,128)(2,1)S(1)}, bf16[6,12288]{1,0:T(8,128)(2,1)S(1)}, u32[]{:S(2)}, u32[]{:S(2)}) collective-permute-start(bf16[6,12288]{1,0:T(8,128)(2,1)S(1)} %get-tuple-element.51), channel_id=1, source_target_pairs={{0,8},{8,16},{16,24},{24,32},{32,40},{40,48},{48,56},{56,64},{64,7... | collective-permute-start | bytes 442376 | tf_op jit(solution)/shard_map/ppermute | solution.py:34
  31.6 34.2 %collective-permute-start.7 = (bf16[128,1024]{1,0:T(8,128)(2,1)S(1)}, bf16[128,1024]{1,0:T(8,128)(2,1)S(1)}, u32[]{:S(2)}, u32[]{:S(2)}) collective-permute-start(bf16[128,1024]{1,0:T(8,128)(2,1)S(1)} %get-tuple-element.66), channel_id=1, source_target_pairs={{0,8},{8,16},{16,24},{24,32},{32,40},{40,48},{48,56},{56,64},{64,7... | collective-permute-start | bytes 786440 | tf_op jit(solution)/shard_map/ppermute | solution.py:34
  32.4 43.4 %collective-permute-start.8 = (bf16[128,1024]{1,0:T(8,128)(2,1)S(1)}, bf16[128,1024]{1,0:T(8,128)(2,1)S(1)}, u32[]{:S(2)}, u32[]{:S(2)}) collective-permute-start(bf16[128,1024]{1,0:T(8,128)(2,1)S(1)} %get-tuple-element.67), channel_id=1, source_target_pairs={{0,248},{8,0},{16,8},{24,16},{32,24},{40,32},{48,40},{56,48},{64,5... | collective-permute-start | bytes 786440 | tf_op jit(solution)/shard_map/ppermute | solution.py:34
  47.5 38.3 %collective-permute-start.5 = (bf16[128,1024]{1,0:T(8,128)(2,1)S(1)}, bf16[128,1024]{1,0:T(8,128)(2,1)S(1)}, u32[]{:S(2)}, u32[]{:S(2)}) collective-permute-start(bf16[128,1024]{1,0:T(8,128)(2,1)S(1)} %get-tuple-element.63), channel_id=1, source_target_pairs={{0,8},{8,16},{16,24},{24,32},{32,40},{40,48},{48,56},{56,64},{64,7... | collective-permute-start | bytes 786440 | tf_op jit(solution)/shard_map/ppermute | solution.py:34
  47.5 48.5 %collective-permute-start.6 = (bf16[128,1024]{1,0:T(8,128)(2,1)S(1)}, bf16[128,1024]{1,0:T(8,128)(2,1)S(1)}, u32[]{:S(2)}, u32[]{:S(2)}) collective-permute-start(bf16[128,1024]{1,0:T(8,128)(2,1)S(1)} %get-tuple-element.64), channel_id=1, source_target_pairs={{0,248},{8,0},{16,8},{24,16},{32,24},{40,32},{48,40},{56,48},{64,5... | collective-permute-start | bytes 786440 | tf_op jit(solution)/shard_map/ppermute | solution.py:34
  61.6 14.2 %copy-start.4 = (f32[3,128,1024]{2,1,0:T(8,128)S(1)}, f32[3,128,1024]{2,1,0:T(8,128)}, u32[]{:S(2)}) copy-start(f32[3,128,1024]{2,1,0:T(8,128)} %get-tuple-element.68.refs_2_) | copy-start | bytes 4718596
  61.6 44.3 %collective-permute-start.3 = (bf16[128,1024]{1,0:T(8,128)(2,1)S(1)}, bf16[128,1024]{1,0:T(8,128)(2,1)S(1)}, u32[]{:S(2)}, u32[]{:S(2)}) collective-permute-start(bf16[128,1024]{1,0:T(8,128)(2,1)S(1)} %get-tuple-element.60), channel_id=1, source_target_pairs={{0,8},{8,16},{16,24},{24,32},{32,40},{40,48},{48,56},{56,64},{64,7... | collective-permute-start | bytes 786440 | tf_op jit(solution)/shard_map/ppermute | solution.py:34
  65.7 40.2 %collective-permute-start.4 = (bf16[128,1024]{1,0:T(8,128)(2,1)S(1)}, bf16[128,1024]{1,0:T(8,128)(2,1)S(1)}, u32[]{:S(2)}, u32[]{:S(2)}) collective-permute-start(bf16[128,1024]{1,0:T(8,128)(2,1)S(1)} %get-tuple-element.61), channel_id=1, source_target_pairs={{0,248},{8,0},{16,8},{24,16},{32,24},{40,32},{48,40},{56,48},{64,5... | collective-permute-start | bytes 786440 | tf_op jit(solution)/shard_map/ppermute | solution.py:34
  75.8 40.1 %collective-permute-start.1 = (bf16[128,1024]{1,0:T(8,128)(2,1)S(1)}, bf16[128,1024]{1,0:T(8,128)(2,1)S(1)}, u32[]{:S(2)}, u32[]{:S(2)}) collective-permute-start(bf16[128,1024]{1,0:T(8,128)(2,1)S(1)} %get-tuple-element.55), channel_id=1, source_target_pairs={{0,8},{8,16},{16,24},{24,32},{32,40},{40,48},{48,56},{56,64},{64,7... | collective-permute-start | bytes 786440 | tf_op jit(solution)/shard_map/ppermute | solution.py:34
  75.8 20.1 %copy-start.3 = (f32[3,128,1024]{2,1,0:T(8,128)S(1)}, f32[3,128,1024]{2,1,0:T(8,128)}, u32[]{:S(2)}) copy-start(f32[3,128,1024]{2,1,0:T(8,128)} %get-tuple-element.65.refs_2_) | copy-start | bytes 4718596
  85.7 35.4 %collective-permute-start.2 = (bf16[128,1024]{1,0:T(8,128)(2,1)S(1)}, bf16[128,1024]{1,0:T(8,128)(2,1)S(1)}, u32[]{:S(2)}, u32[]{:S(2)}) collective-permute-start(bf16[128,1024]{1,0:T(8,128)(2,1)S(1)} %get-tuple-element.56), channel_id=1, source_target_pairs={{0,248},{8,0},{16,8},{24,16},{32,24},{40,32},{48,40},{56,48},{64,5... | collective-permute-start | bytes 786440 | tf_op jit(solution)/shard_map/ppermute | solution.py:34
  95.9 10.0 %copy-start.2 = (f32[3,128,1024]{2,1,0:T(8,128)S(1)}, f32[3,128,1024]{2,1,0:T(8,128)}, u32[]{:S(2)}) copy-start(f32[3,128,1024]{2,1,0:T(8,128)} %get-tuple-element.62.refs_2_) | copy-start | bytes 4718596
  105.9 15.3 %copy-start.1 = (f32[3,128,1024]{2,1,0:T(8,128)S(1)}, f32[3,128,1024]{2,1,0:T(8,128)}, u32[]{:S(2)}) copy-start(f32[3,128,1024]{2,1,0:T(8,128)} %get-tuple-element.57.refs_2_) | copy-start | bytes 4718596
  131.0 54.1 %copy-start = (s32[1,1,4]{2,1,0:T(1,128)S(1)}, s32[1,1,4]{2,1,0:T(1,128)}, u32[]{:S(2)}) copy-start(s32[1,1,4]{2,1,0:T(1,128)} %param.11) | copy-start | bytes 52
  131.9 39.6 %all-to-all-start = ((f32[256,4,128]{2,1,0:T(4,128)}), f32[256,4,128]{2,1,0:T(4,128)S(1)}, u32[]{:S(2)}, u32[]{:S(2)}) async-start(f32[256,4,128]{2,1,0:T(4,128)} %bitcast.13), calls=%async_computation | async-start | bytes 1048576 | tf_op jit(solution)/shard_map/all_to_all | solution.py:554
  151.2 33.9 %collective-permute-start.9 = (bf16[3,8,4096]{2,1,0:T(8,128)(2,1)S(1)}, bf16[3,8,4096]{2,1,0:T(8,128)(2,1)S(1)}, u32[]{:S(2)}, u32[]{:S(2)}) collective-permute-start(bf16[3,8,4096]{2,1,0:T(8,128)(2,1)S(1)} %slice.19), channel_id=1, source_target_pairs={{0,248},{8,0},{16,8},{24,16},{32,24},{40,32},{48,40},{56,48},{64,5... | collective-permute-start | bytes 589832 | tf_op jit(solution)/shard_map/ppermute | solution.py:34
  172.4 25.0 %all-to-all-start.1 = ((f32[32,4,128]{2,1,0:T(4,128)}), f32[32,4,128]{2,1,0:T(4,128)S(1)}, u32[]{:S(2)}, u32[]{:S(2)}) async-start(f32[32,4,128]{2,1,0:T(4,128)} %broadcast_in_dim.18), calls=%async_computation.1 | async-start | bytes 131072 | tf_op jit(solution)/shard_map/all_to_all | solution.py:557

commit v3 on v2

--- a/solution.py
+++ b/solution.py
@@ -430,11 +430,11 @@
     for place in range(3 * BLOCKS):
         part, first = place // BLOCKS, place % BLOCKS * BLK
         own = slice(first, first + BLK)
-        head = head_ref[part, :, own].astype(f32)
-        ahead = jnp.concatenate([jnp.zeros_like(head), head], axis=0)
+        empty = jnp.zeros((8, BLK), f32)
+        ahead = jnp.concatenate([empty, head_ref[part, :, own].astype(f32), empty[: 9 - SHORT]], axis=0)
         first = place % per_shard * PACK
         taps = tap_rows(params_ref[pl.ds(place // per_shard, 1), first : first + PACK])
-        extra = jnp.zeros_like(head)
+        extra = empty
         for lag in range(1, SHORT):
             extra = extra + taps[lag : lag + 1] * ahead[lag : lag + 8]
         final = end_ref[part, :, own] + extra * keep
@@ -539,7 +539,7 @@
             sends, per_shard, kept,
         )
     mixed, grad_source, short_sums, lag_sums, skip_sums, head, end = kept
-    head = ring(head[:, :8], -1)
+    head = ring(head[:, : SHORT - 1], -1)
 
     skip_slabs = C // LANES // shards
     skip_sums = skip_sums.reshape(shards, skip_slabs, 1, LANES)
@@ -551,7 +551,8 @@
     )
     piece = sums.shape[1] // count
     sums = sums.reshape(shards * count, piece, LANES)
-    sums = jnp.sum(lax.all_to_all(sums, ("fsdp", "ctx"), 0, 0, tiled=True), axis=0)
+    sums = lax.all_to_all(sums.astype(bf16), ("fsdp", "ctx"), 0, 0, tiled=True)
+    sums = jnp.sum(sums.astype(f32), axis=0)
     sums = sums * (float(shards * count * TOK) ** -0.5)
     grad_source = patch_call(starts[0], grad_source, end, head, params)
     sums = lax.all_to_all(

time: 200 us -> 192 us (0.960)
  waiting for transfers between devices: 25.4 us -> 20.3 us
  starting transfers between devices: 89 us -> 85 us
    all_to_all x1, waiting for transfers between devices: 10.2 us -> 5.05 us  [body(): sums = lax.all_to_all(sums.astype(bf16), ('fsdp', 'ctx'), 0, 0, tiled=True)]
    all_to_all x1, starting transfers between devices: 12.7 us -> 8.74 us  [body(): lax.all_to_all(jnp.broadcast_to(sums[None], (count,) + sums.shape), 'ctx'...]
  transfers between devices with their start and end apart: 12 -> 12, of which waited for: 3 -> 3; matrix products, arithmetic and copies ran while one was open for 0% -> 0% of each run, Pallas kernels for 24% -> 25%
where the time goes in v3:
time: 192 us; the launch traced here: 190 us
  starting transfers between devices  85 us (44%)
  Pallas kernels  62.7 us (33%)
  waiting for transfers between devices  20.3 us (11%)
  blocking collectives  17.7 us (9%)
  local copies, waits for them, and re-layouts  2.55 us (1%)
    ppermute x10, starting transfers between devices, ring(): lax.ppermute(block, 'ctx', [(i, (i + distance) % count) for i in range(co...  57.1 us
    pallas_call x4, Pallas kernels, main_call(): pl.pallas_call(kernel, grid=(count,), in_specs=in_specs, out_specs=[first...  39.6 us
    all_to_all x1, starting transfers between devices, body(): sums = lax.all_to_all(sums.astype(bf16), ('fsdp', 'ctx'), 0, 0, tiled=True)  19.3 us
    all_gather x1, blocking collectives, body(): params = lax.all_gather(packed, 'fsdp', axis=0)  17.7 us
    pallas_call x4, Pallas kernels, feature_call(): pl.pallas_call(feature_kernel, grid=(count,), in_specs=[pl.BlockSpec((TOK...  16 us
    all_to_all x1, waiting for transfers between devices, body(): lax.all_to_all(jnp.broadcast_to(sums[None], (count,) + sums.shape), 'ctx'...  9.97 us
    all_to_all x1, starting transfers between devices, body(): lax.all_to_all(jnp.broadcast_to(sums[None], (count,) + sums.shape), 'ctx'...  8.74 us
    ppermute x10, waiting for transfers between devices, ring(): lax.ppermute(block, 'ctx', [(i, (i + distance) % count) for i in range(co...  5.32 us
  transfers between devices with their start and end apart: 12, of which 3 were waited for; matrix products, arithmetic and copies ran while one was open for 0% of the time, Pallas kernels for 25%

profile of v3, /device:TPU:32, one launch (start us, length us, event | category | flops | bytes accessed | tf_op | source)
XLA Modules:
  0.0 190.2 jit_solution(2104637711440172746)
XLA Ops:
  0.6 1.3 prepare.1
  1.9 6.4 %collective-permute-start = (bf16[6,12288]{1,0:T(8,128)(2,1)S(1)}, bf16[6,12288]{1,0:T(8,128)(2,1)S(1)}, u32[]{:S(2)}, u32[]{:S(2)}) collective-permute-start(bf16[6,12288]{1,0:T(8,128)(2,1)S(1)} %get-tuple-element.51), channel_id=1, source_target_pairs={{0,8},{8,16},{16,24},{24,32},{32,40},{40,48},{48,56},{56,64},{64,7... | collective-permute-start | bytes 442376 | tf_op jit(solution)/shard_map/ppermute | solution.py:34
  8.3 1.7 shifts.1
  9.9 17.7 %all-gather = f32[1024,128]{1,0:T(8,128)S(1)} all-gather(f32[128,128]{1,0:T(8,128)S(1)} %get-tuple-element.52), channel_id=2, replica_groups=mesh['ctx'=32,'fsdp'=8] {'fsdp'}, dimensions={0}, use_global_device_ids=true | all-gather | bytes 589824 | tf_op jit(solution)/shard_map/all_gather | solution.py:528
  27.6 0.0 collective-permute-done.tq.tk.tv.refs_7_.refs_8_.refs_9_
  27.6 3.9 %features.7 = (bf16[128,1024]{1,0:T(8,128)(2,1)S(1)}, bf16[128,1024]{1,0:T(8,128)(2,1)S(1)}, f32[3,128,1024]{2,1,0:T(8,128)}) custom-call(bf16[128,12288]{1,0:T(8,128)(2,1)} %bitcast.64, bf16[128,12288]{1,0:T(8,128)(2,1)} %bitcast.65, bf16[128,12288]{1,0:T(8,128)(2,1)} %bitcast.66, ...), custom_call_target="tpu_custom_call" | custom-call | flops 679477248 | bytes 1572864 | tf_op jit(solution)/shard_map/features/pallas_call | solution.py:176
  31.6 0.8 collective-permute-start.7
  32.4 9.3 %collective-permute-start.8 = (bf16[128,1024]{1,0:T(8,128)(2,1)S(1)}, bf16[128,1024]{1,0:T(8,128)(2,1)S(1)}, u32[]{:S(2)}, u32[]{:S(2)}) collective-permute-start(bf16[128,1024]{1,0:T(8,128)(2,1)S(1)} %get-tuple-element.67), channel_id=1, source_target_pairs={{0,248},{8,0},{16,8},{24,16},{32,24},{40,32},{48,40},{56,48},{64,5... | collective-permute-start | bytes 786440 | tf_op jit(solution)/shard_map/ppermute | solution.py:34
  41.7 1.8 links.1
  43.5 4.0 %features.6 = (bf16[128,1024]{1,0:T(8,128)(2,1)S(1)}, bf16[128,1024]{1,0:T(8,128)(2,1)S(1)}, f32[3,128,1024]{2,1,0:T(8,128)}) custom-call(bf16[128,12288]{1,0:T(8,128)(2,1)} %bitcast.67, bf16[128,12288]{1,0:T(8,128)(2,1)} %bitcast.68, bf16[128,12288]{1,0:T(8,128)(2,1)} %bitcast.69, ...), custom_call_target="tpu_custom_call" | custom-call | flops 679477248 | bytes 1572864 | tf_op jit(solution)/shard_map/features/pallas_call | solution.py:176
  47.5 0.0 collective-permute-start.5
  47.5 10.1 %collective-permute-start.6 = (bf16[128,1024]{1,0:T(8,128)(2,1)S(1)}, bf16[128,1024]{1,0:T(8,128)(2,1)S(1)}, u32[]{:S(2)}, u32[]{:S(2)}) collective-permute-start(bf16[128,1024]{1,0:T(8,128)(2,1)S(1)} %get-tuple-element.64), channel_id=1, source_target_pairs={{0,248},{8,0},{16,8},{24,16},{32,24},{40,32},{48,40},{56,48},{64,5... | collective-permute-start | bytes 786440 | tf_op jit(solution)/shard_map/ppermute | solution.py:34
  57.6 4.0 %features.5 = (bf16[128,1024]{1,0:T(8,128)(2,1)S(1)}, bf16[128,1024]{1,0:T(8,128)(2,1)S(1)}, f32[3,128,1024]{2,1,0:T(8,128)}) custom-call(bf16[128,12288]{1,0:T(8,128)(2,1)} %bitcast.70, bf16[128,12288]{1,0:T(8,128)(2,1)} %bitcast.71, bf16[128,12288]{1,0:T(8,128)(2,1)} %bitcast.72, ...), custom_call_target="tpu_custom_call" | custom-call | flops 679477248 | bytes 1572864 | tf_op jit(solution)/shard_map/features/pallas_call | solution.py:176
  61.6 0.0 copy-start.4
  61.6 0.0 collective-permute-start.3
  61.6 4.1 %features.4 = (bf16[128,1024]{1,0:T(8,128)(2,1)S(1)}, bf16[128,1024]{1,0:T(8,128)(2,1)S(1)}, f32[3,128,1024]{2,1,0:T(8,128)}) custom-call(bf16[128,12288]{1,0:T(8,128)(2,1)} %bitcast.75, bf16[128,12288]{1,0:T(8,128)(2,1)} %bitcast.74, bf16[128,12288]{1,0:T(8,128)(2,1)} %bitcast.73, ...), custom_call_target="tpu_custom_call" | custom-call | flops 679477248 | bytes 1572864 | tf_op jit(solution)/shard_map/features/pallas_call | solution.py:176
  65.7 0.0 collective-permute-done.7.refs_0_
  65.7 10.1 %collective-permute-start.4 = (bf16[128,1024]{1,0:T(8,128)(2,1)S(1)}, bf16[128,1024]{1,0:T(8,128)(2,1)S(1)}, u32[]{:S(2)}, u32[]{:S(2)}) collective-permute-start(bf16[128,1024]{1,0:T(8,128)(2,1)S(1)} %get-tuple-element.61), channel_id=1, source_target_pairs={{0,248},{8,0},{16,8},{24,16},{32,24},{40,32},{48,40},{56,48},{64,5... | collective-permute-start | bytes 786440 | tf_op jit(solution)/shard_map/ppermute | solution.py:34
  75.8 0.0 collective-permute-done.8.refs_1_
  75.8 0.0 collective-permute-start.1
  75.8 0.0 copy-done.4
  75.8 0.0 copy-start.3
  75.8 9.9 %main.4 = (bf16[128,4096]{1,0:T(8,128)(2,1)}, bf16[128,12288]{1,0:T(8,128)(2,1)}, f32[3,32,8,128]{3,2,1,0:T(8,128)S(1)}, f32[256,128]{1,0:T(8,128)S(1)}, f32[32,...) custom-call(bf16[128,1024]{1,0:T(8,128)(2,1)S(1)} %collective-permute-done.7.refs_0_, ...), custom_call_target="tpu_custom_call" | custom-call | flops 10000000000 | bytes 5242880 | tf_op jit(solution)/shard_map/main/pallas_call | solution.py:379
  85.7 0.0 collective-permute-done.5.refs_0_
  85.7 10.2 %collective-permute-start.2 = (bf16[128,1024]{1,0:T(8,128)(2,1)S(1)}, bf16[128,1024]{1,0:T(8,128)(2,1)S(1)}, u32[]{:S(2)}, u32[]{:S(2)}) collective-permute-start(bf16[128,1024]{1,0:T(8,128)(2,1)S(1)} %get-tuple-element.56), channel_id=1, source_target_pairs={{0,248},{8,0},{16,8},{24,16},{32,24},{40,32},{48,40},{56,48},{64,5... | collective-permute-start | bytes 786440 | tf_op jit(solution)/shard_map/ppermute | solution.py:34
  95.9 0.0 collective-permute-done.6.refs_1_
  95.9 0.0 copy-done.3
  95.9 0.0 copy-start.2
  96.0 9.9 %main.5 = (bf16[128,4096]{1,0:T(8,128)(2,1)}, bf16[128,12288]{1,0:T(8,128)(2,1)}, f32[3,32,8,128]{3,2,1,0:T(8,128)S(1)}, f32[256,128]{1,0:T(8,128)S(1)}, f32[32,...) custom-call(bf16[128,1024]{1,0:T(8,128)(2,1)S(1)} %collective-permut, ...), custom_call_target="tpu_custom_call", output_to_operand_aliasing={{0}: (18, {}), {1}: (19, {}), {2}: (20, {}), {3}: (21, {}),... | custom-call | flops 10000000000 | bytes 5242880 | tf_op jit(solution)/shard_map/main/pallas_call | solution.py:379
  105.9 0.0 collective-permute-done.3.refs_0_
  105.9 0.0 collective-permute-done.4.refs_1_
  105.9 0.0 copy-done.2
  105.9 0.0 copy-start.1
  105.9 9.9 %main.6 = (bf16[128,4096]{1,0:T(8,128)(2,1)}, bf16[128,12288]{1,0:T(8,128)(2,1)}, f32[3,32,8,128]{3,2,1,0:T(8,128)S(1)}, f32[256,128]{1,0:T(8,128)S(1)}, f32[32,...) custom-call(bf16[128,1024]{1,0:T(8,128)(2,1)S(1)} %collective-permut, ...), custom_call_target="tpu_custom_call", output_to_operand_aliasing={{0}: (18, {}), {1}: (19, {}), {2}: (20, {}), {3}: (21, {}),... | custom-call | flops 10000000000 | bytes 5242880 | tf_op jit(solution)/shard_map/main/pallas_call | solution.py:379
  115.9 0.0 collective-permute-done.1.refs_0_
  115.9 5.3 %collective-permute-done.2.refs_1_ = bf16[128,1024]{1,0:T(8,128)(2,1)S(1)} collective-permute-done((bf16[128,1024]{1,0:T(8,128)(2,1)S(1)}, bf16[128,1024]{1,0:T(8,128)(2,1)S(1)}, u32[]{:S(2)}, u32[]{:S(2)}) %collective-permute-start.2) | collective-permute-done | bytes 262176 | tf_op jit(solution)/shard_map/ppermute | solution.py:34
  121.2 0.0 copy-done.1
  121.2 0.0 copy-start
  121.2 9.8 %main.7 = (bf16[128,4096]{1,0:T(8,128)(2,1)}, bf16[128,12288]{1,0:T(8,128)(2,1)}, f32[3,32,8,128]{3,2,1,0:T(8,128)S(1)}, f32[256,128]{1,0:T(8,128)S(1)}, f32[32,...) custom-call(bf16[128,1024]{1,0:T(8,128)(2,1)S(1)} %collective-permut, ...), custom_call_target="tpu_custom_call", output_to_operand_aliasing={{0}: (18, {}), {1}: (19, {}), {2}: (20, {}), {3}: (21, {}),... | custom-call | flops 10000000000 | bytes 5242880 | tf_op jit(solution)/shard_map/main/pallas_call | solution.py:379
  131.1 0.7 pad_maximum_fusion
  131.8 19.3 %all-to-all-start = ((bf16[256,4,128]{2,1,0:T(4,128)(2,1)}), bf16[256,4,128]{2,1,0:T(4,128)(2,1)S(1)}, u32[]{:S(2)}, u32[]{:S(2)}) async-start(bf16[256,4,128]{2,1,0:T(4,128)(2,1)} %bitcast.13), calls=%async_computation | async-start | bytes 524288 | tf_op jit(solution)/shard_map/all_to_all | solution.py:554
  151.1 10.1 %collective-permute-start.9 = (bf16[3,6,4096]{2,1,0:T(8,128)(2,1)S(1)}, bf16[3,6,4096]{2,1,0:T(8,128)(2,1)S(1)}, u32[]{:S(2)}, u32[]{:S(2)}) collective-permute-start(bf16[3,6,4096]{2,1,0:T(8,128)(2,1)S(1)} %slice.19), channel_id=1, source_target_pairs={{0,248},{8,0},{16,8},{24,16},{32,24},{40,32},{48,40},{56,48},{64,5... | collective-permute-start | bytes 442376 | tf_op jit(solution)/shard_map/ppermute | solution.py:34
  161.2 5.1 %all-to-all-done = bf16[256,4,128]{2,1,0:T(4,128)(2,1)S(1)} async-done(((bf16[256,4,128]{2,1,0:T(4,128)(2,1)}), bf16[256,4,128]{2,1,0:T(4,128)(2,1)S(1)}, u32[]{:S(2)}, u32[]{:S(2)}) %all-to-all-start) | async-done | bytes 262176 | tf_op jit(solution)/shard_map/all_to_all | solution.py:554
  166.2 0.3 convert_reduce_fusion
  166.5 0.6 broadcast_in_dim.18
  167.1 8.7 %all-to-all-start.1 = ((f32[32,4,128]{2,1,0:T(4,128)}), f32[32,4,128]{2,1,0:T(4,128)S(1)}, u32[]{:S(2)}, u32[]{:S(2)}) async-start(f32[32,4,128]{2,1,0:T(4,128)} %broadcast_in_dim.18), calls=%async_computation.1 | async-start | bytes 131072 | tf_op jit(solution)/shard_map/all_to_all | solution.py:558
  175.9 0.0 collective-permute-done.9.head_ref
  175.9 0.0 copy-done
  175.9 2.4 %patch.1 = bf16[128,12288]{1,0:T(8,128)(2,1)} custom-call(s32[1,4]{1,0:T(1,128)S(1)} %bitcast.62, bf16[128,12288]{1,0:T(8,128)(2,1)} %get-tuple-element.91.source_ref, f32[3,8,4096]{2,1,0:T(8,128)S(1)} %get-tuple-element.92.end_ref, bf16[3,6,4096]{2,1,0:T(8,128)(2,1)S(1)} %collective-permute-done.9.head_ref, ...), custom_call_target="tpu_custom_call", output_to_operand_aliasing={{}: (1, {})} | custom-call | flops 1000000 | bytes 2000000 | tf_op jit(solution)/shard_map/patch/pallas_call | solution.py:453
  178.3 10.0 %all-to-all-done.1 = f32[32,4,128]{2,1,0:T(4,128)S(1)} async-done(((f32[32,4,128]{2,1,0:T(4,128)}), f32[32,4,128]{2,1,0:T(4,128)S(1)}, u32[]{:S(2)}, u32[]{:S(2)}) %all-to-all-start.1) | async-done | bytes 65568 | tf_op jit(solution)/shard_map/all_to_all | solution.py:558
  188.3 0.6 slice_bitcast_fusion
  188.9 0.6 slice.28
  189.5 0.7 rev.3
  (6 shorter events, 0.1 us)
Async XLA Ops:
  1.9 25.7 %collective-permute-start = (bf16[6,12288]{1,0:T(8,128)(2,1)S(1)}, bf16[6,12288]{1,0:T(8,128)(2,1)S(1)}, u32[]{:S(2)}, u32[]{:S(2)}) collective-permute-start(bf16[6,12288]{1,0:T(8,128)(2,1)S(1)} %get-tuple-element.51), channel_id=1, source_target_pairs={{0,8},{8,16},{16,24},{24,32},{32,40},{40,48},{48,56},{56,64},{64,7... | collective-permute-start | bytes 442376 | tf_op jit(solution)/shard_map/ppermute | solution.py:34
  31.6 34.2 %collective-permute-start.7 = (bf16[128,1024]{1,0:T(8,128)(2,1)S(1)}, bf16[128,1024]{1,0:T(8,128)(2,1)S(1)}, u32[]{:S(2)}, u32[]{:S(2)}) collective-permute-start(bf16[128,1024]{1,0:T(8,128)(2,1)S(1)} %get-tuple-element.66), channel_id=1, source_target_pairs={{0,8},{8,16},{16,24},{24,32},{32,40},{40,48},{48,56},{56,64},{64,7... | collective-permute-start | bytes 786440 | tf_op jit(solution)/shard_map/ppermute | solution.py:34
  32.4 43.4 %collective-permute-start.8 = (bf16[128,1024]{1,0:T(8,128)(2,1)S(1)}, bf16[128,1024]{1,0:T(8,128)(2,1)S(1)}, u32[]{:S(2)}, u32[]{:S(2)}) collective-permute-start(bf16[128,1024]{1,0:T(8,128)(2,1)S(1)} %get-tuple-element.67), channel_id=1, source_target_pairs={{0,248},{8,0},{16,8},{24,16},{32,24},{40,32},{48,40},{56,48},{64,5... | collective-permute-start | bytes 786440 | tf_op jit(solution)/shard_map/ppermute | solution.py:34
  47.5 38.3 %collective-permute-start.5 = (bf16[128,1024]{1,0:T(8,128)(2,1)S(1)}, bf16[128,1024]{1,0:T(8,128)(2,1)S(1)}, u32[]{:S(2)}, u32[]{:S(2)}) collective-permute-start(bf16[128,1024]{1,0:T(8,128)(2,1)S(1)} %get-tuple-element.63), channel_id=1, source_target_pairs={{0,8},{8,16},{16,24},{24,32},{32,40},{40,48},{48,56},{56,64},{64,7... | collective-permute-start | bytes 786440 | tf_op jit(solution)/shard_map/ppermute | solution.py:34
  47.5 48.5 %collective-permute-start.6 = (bf16[128,1024]{1,0:T(8,128)(2,1)S(1)}, bf16[128,1024]{1,0:T(8,128)(2,1)S(1)}, u32[]{:S(2)}, u32[]{:S(2)}) collective-permute-start(bf16[128,1024]{1,0:T(8,128)(2,1)S(1)} %get-tuple-element.64), channel_id=1, source_target_pairs={{0,248},{8,0},{16,8},{24,16},{32,24},{40,32},{48,40},{56,48},{64,5... | collective-permute-start | bytes 786440 | tf_op jit(solution)/shard_map/ppermute | solution.py:34
  61.6 14.2 %copy-start.4 = (f32[3,128,1024]{2,1,0:T(8,128)S(1)}, f32[3,128,1024]{2,1,0:T(8,128)}, u32[]{:S(2)}) copy-start(f32[3,128,1024]{2,1,0:T(8,128)} %get-tuple-element.68.refs_2_) | copy-start | bytes 4718596
  61.6 44.3 %collective-permute-start.3 = (bf16[128,1024]{1,0:T(8,128)(2,1)S(1)}, bf16[128,1024]{1,0:T(8,128)(2,1)S(1)}, u32[]{:S(2)}, u32[]{:S(2)}) collective-permute-start(bf16[128,1024]{1,0:T(8,128)(2,1)S(1)} %get-tuple-element.60), channel_id=1, source_target_pairs={{0,8},{8,16},{16,24},{24,32},{32,40},{40,48},{48,56},{56,64},{64,7... | collective-permute-start | bytes 786440 | tf_op jit(solution)/shard_map/ppermute | solution.py:34
  65.7 40.2 %collective-permute-start.4 = (bf16[128,1024]{1,0:T(8,128)(2,1)S(1)}, bf16[128,1024]{1,0:T(8,128)(2,1)S(1)}, u32[]{:S(2)}, u32[]{:S(2)}) collective-permute-start(bf16[128,1024]{1,0:T(8,128)(2,1)S(1)} %get-tuple-element.61), channel_id=1, source_target_pairs={{0,248},{8,0},{16,8},{24,16},{32,24},{40,32},{48,40},{56,48},{64,5... | collective-permute-start | bytes 786440 | tf_op jit(solution)/shard_map/ppermute | solution.py:34
  75.8 40.1 %collective-permute-start.1 = (bf16[128,1024]{1,0:T(8,128)(2,1)S(1)}, bf16[128,1024]{1,0:T(8,128)(2,1)S(1)}, u32[]{:S(2)}, u32[]{:S(2)}) collective-permute-start(bf16[128,1024]{1,0:T(8,128)(2,1)S(1)} %get-tuple-element.55), channel_id=1, source_target_pairs={{0,8},{8,16},{16,24},{24,32},{32,40},{40,48},{48,56},{56,64},{64,7... | collective-permute-start | bytes 786440 | tf_op jit(solution)/shard_map/ppermute | solution.py:34
  75.8 20.1 %copy-start.3 = (f32[3,128,1024]{2,1,0:T(8,128)S(1)}, f32[3,128,1024]{2,1,0:T(8,128)}, u32[]{:S(2)}) copy-start(f32[3,128,1024]{2,1,0:T(8,128)} %get-tuple-element.65.refs_2_) | copy-start | bytes 4718596
  85.7 35.4 %collective-permute-start.2 = (bf16[128,1024]{1,0:T(8,128)(2,1)S(1)}, bf16[128,1024]{1,0:T(8,128)(2,1)S(1)}, u32[]{:S(2)}, u32[]{:S(2)}) collective-permute-start(bf16[128,1024]{1,0:T(8,128)(2,1)S(1)} %get-tuple-element.56), channel_id=1, source_target_pairs={{0,248},{8,0},{16,8},{24,16},{32,24},{40,32},{48,40},{56,48},{64,5... | collective-permute-start | bytes 786440 | tf_op jit(solution)/shard_map/ppermute | solution.py:34
  95.9 10.0 %copy-start.2 = (f32[3,128,1024]{2,1,0:T(8,128)S(1)}, f32[3,128,1024]{2,1,0:T(8,128)}, u32[]{:S(2)}) copy-start(f32[3,128,1024]{2,1,0:T(8,128)} %get-tuple-element.62.refs_2_) | copy-start | bytes 4718596
  105.9 15.3 %copy-start.1 = (f32[3,128,1024]{2,1,0:T(8,128)S(1)}, f32[3,128,1024]{2,1,0:T(8,128)}, u32[]{:S(2)}) copy-start(f32[3,128,1024]{2,1,0:T(8,128)} %get-tuple-element.57.refs_2_) | copy-start | bytes 4718596
  121.2 54.7 %copy-start = (s32[1,1,4]{2,1,0:T(1,128)S(1)}, s32[1,1,4]{2,1,0:T(1,128)}, u32[]{:S(2)}) copy-start(s32[1,1,4]{2,1,0:T(1,128)} %param.11) | copy-start | bytes 52
  131.8 34.4 %all-to-all-start = ((bf16[256,4,128]{2,1,0:T(4,128)(2,1)}), bf16[256,4,128]{2,1,0:T(4,128)(2,1)S(1)}, u32[]{:S(2)}, u32[]{:S(2)}) async-start(bf16[256,4,128]{2,1,0:T(4,128)(2,1)} %bitcast.13), calls=%async_computation | async-start | bytes 524288 | tf_op jit(solution)/shard_map/all_to_all | solution.py:554
  151.1 24.8 %collective-permute-start.9 = (bf16[3,6,4096]{2,1,0:T(8,128)(2,1)S(1)}, bf16[3,6,4096]{2,1,0:T(8,128)(2,1)S(1)}, u32[]{:S(2)}, u32[]{:S(2)}) collective-permute-start(bf16[3,6,4096]{2,1,0:T(8,128)(2,1)S(1)} %slice.19), channel_id=1, source_target_pairs={{0,248},{8,0},{16,8},{24,16},{32,24},{40,32},{48,40},{56,48},{64,5... | collective-permute-start | bytes 442376 | tf_op jit(solution)/shard_map/ppermute | solution.py:34
  167.1 21.1 %all-to-all-start.1 = ((f32[32,4,128]{2,1,0:T(4,128)}), f32[32,4,128]{2,1,0:T(4,128)S(1)}, u32[]{:S(2)}, u32[]{:S(2)}) async-start(f32[32,4,128]{2,1,0:T(4,128)} %broadcast_in_dim.18), calls=%async_computation.1 | async-start | bytes 131072 | tf_op jit(solution)/shard_map/all_to_all | solution.py:558

commit v4 on v3

--- a/solution.py
+++ b/solution.py
@@ -267,7 +267,7 @@
             sums.append(jnp.sum(kept, axis=0, keepdims=True))
         long_out_ref[:, lanes] = out
         gate_grad_ref[:, lanes] = spread
-        lag_ref[rows, :] = jnp.concatenate(sums, axis=0)
+        lag_ref[rows, :] = dot(jnp.concatenate(sums, axis=0).astype(bf16), mask_ref[6])
         return carry
 
     lax.fori_loop(0, SLABS, slab, 0, unroll=UNROLL)
@@ -356,7 +356,7 @@
 
     groups = BLK // GROUP
     operands = [gate_halo, long_halo, feats, in_hbm(grad_out), *[in_hbm(proj)] * 3, tail, tail, tail,
-                params, params, params, params, params, *[in_hbm(table) for table in (masks, unshifts, sends)]]
+                params, params, params, params, params, masks, unshifts, sends]
     in_specs = (
         [local, local, pl.BlockSpec((3, TOK, BLK), lambda j: (0, 0, j)), first_cols]
         + [cols(TOK, part) for part in range(3)]
@@ -562,7 +562,7 @@
     grad_short = sums[: slabs * 8].reshape(slabs, 8, LANES)
     grad_skip = grad_short[:skip_slabs, 7].reshape(-1)
     grad_short = grad_short[:, :SHORT].transpose(1, 0, 2).reshape(SHORT, -1)
-    grad_long = sums[slabs * 8 :, ::-1].T
+    grad_long = sums[slabs * 8 :].T
     return mixed[None], grad_source[None], grad_short, grad_long, grad_skip
 
 

time: 192 us -> 197 us (1.026)
  Pallas kernels: 62.7 us -> 72.4 us
  waiting for transfers between devices: 20.3 us -> 16.9 us
    pallas_call x4, Pallas kernels: 39.6 us -> 49.4 us  [main_call(): pl.pallas_call(kernel, grid=(count,), in_specs=in_specs, out_specs=[first...]
    ppermute x10, waiting for transfers between devices: 5.32 us -> 0.03 us  [ring(): lax.ppermute(block, 'ctx', [(i, (i + distance) % count) for i in range(co...]
  transfers between devices with their start and end apart: 12 -> 12, of which waited for: 3 -> 2; matrix products, arithmetic and copies ran while one was open for 0% -> 0% of each run, Pallas kernels for 25% -> 28%
where the time goes in v4:
time: 197 us; the launch traced here: 196 us
  starting transfers between devices  84.4 us (43%)
  Pallas kernels  72.4 us (37%)
  blocking collectives  17.7 us (9%)
  waiting for transfers between devices  16.9 us (9%)
  local copies, waits for them, and re-layouts  2.5 us (1%)
    ppermute x10, starting transfers between devices, ring(): lax.ppermute(block, 'ctx', [(i, (i + distance) % count) for i in range(co...  57.1 us
    pallas_call x4, Pallas kernels, main_call(): pl.pallas_call(kernel, grid=(count,), in_specs=in_specs, out_specs=[first...  49.4 us
    all_to_all x1, starting transfers between devices, body(): sums = lax.all_to_all(sums.astype(bf16), ('fsdp', 'ctx'), 0, 0, tiled=True)  20 us
    all_gather x1, blocking collectives, body(): params = lax.all_gather(packed, 'fsdp', axis=0)  17.7 us
    pallas_call x4, Pallas kernels, feature_call(): pl.pallas_call(feature_kernel, grid=(count,), in_specs=[pl.BlockSpec((TOK...  15.9 us
    all_to_all x1, waiting for transfers between devices, body(): lax.all_to_all(jnp.broadcast_to(sums[None], (count,) + sums.shape), 'ctx'...  10.3 us
    all_to_all x1, starting transfers between devices, body(): lax.all_to_all(jnp.broadcast_to(sums[None], (count,) + sums.shape), 'ctx'...  7.21 us
    all_to_all x1, waiting for transfers between devices, body(): sums = lax.all_to_all(sums.astype(bf16), ('fsdp', 'ctx'), 0, 0, tiled=True)  6.59 us
  transfers between devices with their start and end apart: 12, of which 2 were waited for; matrix products, arithmetic and copies ran while one was open for 0% of the time, Pallas kernels for 28%

profile of v4, /device:TPU:32, one launch (start us, length us, event | category | flops | bytes accessed | tf_op | source)
XLA Modules:
  0.0 195.8 jit_solution(12127513520007542142)
XLA Ops:
  0.6 1.3 prepare.1
  1.9 6.4 %collective-permute-start = (bf16[6,12288]{1,0:T(8,128)(2,1)S(1)}, bf16[6,12288]{1,0:T(8,128)(2,1)S(1)}, u32[]{:S(2)}, u32[]{:S(2)}) collective-permute-start(bf16[6,12288]{1,0:T(8,128)(2,1)S(1)} %get-tuple-element.51), channel_id=1, source_target_pairs={{0,8},{8,16},{16,24},{24,32},{32,40},{40,48},{48,56},{56,64},{64,7... | collective-permute-start | bytes 442376 | tf_op jit(solution)/shard_map/ppermute | solution.py:34
  8.3 1.7 shifts.1
  9.9 17.7 %all-gather = f32[1024,128]{1,0:T(8,128)S(1)} all-gather(f32[128,128]{1,0:T(8,128)S(1)} %get-tuple-element.52), channel_id=2, replica_groups=mesh['ctx'=32,'fsdp'=8] {'fsdp'}, dimensions={0}, use_global_device_ids=true | all-gather | bytes 589824 | tf_op jit(solution)/shard_map/all_gather | solution.py:528
  27.6 0.0 collective-permute-done.tq.tk.tv.refs_7_.refs_8_.refs_9_
  27.6 3.9 %features.7 = (bf16[128,1024]{1,0:T(8,128)(2,1)S(1)}, bf16[128,1024]{1,0:T(8,128)(2,1)S(1)}, f32[3,128,1024]{2,1,0:T(8,128)}) custom-call(bf16[128,12288]{1,0:T(8,128)(2,1)} %bitcast.65, bf16[128,12288]{1,0:T(8,128)(2,1)} %bitcast.66, bf16[128,12288]{1,0:T(8,128)(2,1)} %bitcast.67, ...), custom_call_target="tpu_custom_call" | custom-call | flops 679477248 | bytes 1572864 | tf_op jit(solution)/shard_map/features/pallas_call | solution.py:176
  31.6 0.8 collective-permute-start.7
  32.4 9.3 %collective-permute-start.8 = (bf16[128,1024]{1,0:T(8,128)(2,1)S(1)}, bf16[128,1024]{1,0:T(8,128)(2,1)S(1)}, u32[]{:S(2)}, u32[]{:S(2)}) collective-permute-start(bf16[128,1024]{1,0:T(8,128)(2,1)S(1)} %get-tuple-element.67), channel_id=1, source_target_pairs={{0,248},{8,0},{16,8},{24,16},{32,24},{40,32},{48,40},{56,48},{64,5... | collective-permute-start | bytes 786440 | tf_op jit(solution)/shard_map/ppermute | solution.py:34
  41.7 1.8 links.1
  43.5 4.0 %features.6 = (bf16[128,1024]{1,0:T(8,128)(2,1)S(1)}, bf16[128,1024]{1,0:T(8,128)(2,1)S(1)}, f32[3,128,1024]{2,1,0:T(8,128)}) custom-call(bf16[128,12288]{1,0:T(8,128)(2,1)} %bitcast.68, bf16[128,12288]{1,0:T(8,128)(2,1)} %bitcast.69, bf16[128,12288]{1,0:T(8,128)(2,1)} %bitcast.70, ...), custom_call_target="tpu_custom_call" | custom-call | flops 679477248 | bytes 1572864 | tf_op jit(solution)/shard_map/features/pallas_call | solution.py:176
  47.5 0.0 collective-permute-start.5
  47.5 10.1 %collective-permute-start.6 = (bf16[128,1024]{1,0:T(8,128)(2,1)S(1)}, bf16[128,1024]{1,0:T(8,128)(2,1)S(1)}, u32[]{:S(2)}, u32[]{:S(2)}) collective-permute-start(bf16[128,1024]{1,0:T(8,128)(2,1)S(1)} %get-tuple-element.64), channel_id=1, source_target_pairs={{0,248},{8,0},{16,8},{24,16},{32,24},{40,32},{48,40},{56,48},{64,5... | collective-permute-start | bytes 786440 | tf_op jit(solution)/shard_map/ppermute | solution.py:34
  57.6 3.9 %features.5 = (bf16[128,1024]{1,0:T(8,128)(2,1)S(1)}, bf16[128,1024]{1,0:T(8,128)(2,1)S(1)}, f32[3,128,1024]{2,1,0:T(8,128)}) custom-call(bf16[128,12288]{1,0:T(8,128)(2,1)} %bitcast.71, bf16[128,12288]{1,0:T(8,128)(2,1)} %bitcast.72, bf16[128,12288]{1,0:T(8,128)(2,1)} %bitcast.73, ...), custom_call_target="tpu_custom_call" | custom-call | flops 679477248 | bytes 1572864 | tf_op jit(solution)/shard_map/features/pallas_call | solution.py:176
  61.6 0.0 copy-start
  61.6 0.0 copy-start.5
  61.6 0.0 copy-start.6
  61.6 0.0 copy-start.7
  61.6 0.1 collective-permute-start.3
  61.7 4.1 %features.4 = (bf16[128,1024]{1,0:T(8,128)(2,1)S(1)}, bf16[128,1024]{1,0:T(8,128)(2,1)S(1)}, f32[3,128,1024]{2,1,0:T(8,128)}) custom-call(bf16[128,12288]{1,0:T(8,128)(2,1)} %bitcast.76, bf16[128,12288]{1,0:T(8,128)(2,1)} %bitcast.75, bf16[128,12288]{1,0:T(8,128)(2,1)} %bitcast.74, ...), custom_call_target="tpu_custom_call" | custom-call | flops 679477248 | bytes 1572864 | tf_op jit(solution)/shard_map/features/pallas_call | solution.py:176
  65.8 0.0 collective-permute-done.7.refs_0_
  65.8 10.1 %collective-permute-start.4 = (bf16[128,1024]{1,0:T(8,128)(2,1)S(1)}, bf16[128,1024]{1,0:T(8,128)(2,1)S(1)}, u32[]{:S(2)}, u32[]{:S(2)}) collective-permute-start(bf16[128,1024]{1,0:T(8,128)(2,1)S(1)} %get-tuple-element.61), channel_id=1, source_target_pairs={{0,248},{8,0},{16,8},{24,16},{32,24},{40,32},{48,40},{56,48},{64,5... | collective-permute-start | bytes 786440 | tf_op jit(solution)/shard_map/ppermute | solution.py:34
  75.8 0.0 collective-permute-done.8.refs_1_
  75.8 0.0 collective-permute-start.1
  75.8 0.0 copy-done
  75.8 0.0 copy-done.5
  75.8 0.0 copy-done.6
  75.9 0.0 copy-done.7
  75.9 0.0 copy-start.4
  75.9 12.3 %main.4 = (bf16[128,4096]{1,0:T(8,128)(2,1)}, bf16[128,12288]{1,0:T(8,128)(2,1)}, f32[3,32,8,128]{3,2,1,0:T(8,128)S(1)}, f32[256,128]{1,0:T(8,128)S(1)}, f32[32,...) custom-call(bf16[128,1024]{1,0:T(8,128)(2,1)S(1)} %collective-permute-done.7.refs_0_, ...), custom_call_target="tpu_custom_call" | custom-call | flops 10000000000 | bytes 5242880 | tf_op jit(solution)/shard_map/main/pallas_call | solution.py:379
  88.2 0.0 collective-permute-done.5.refs_0_
  88.2 10.2 %collective-permute-start.2 = (bf16[128,1024]{1,0:T(8,128)(2,1)S(1)}, bf16[128,1024]{1,0:T(8,128)(2,1)S(1)}, u32[]{:S(2)}, u32[]{:S(2)}) collective-permute-start(bf16[128,1024]{1,0:T(8,128)(2,1)S(1)} %get-tuple-element.56), channel_id=1, source_target_pairs={{0,248},{8,0},{16,8},{24,16},{32,24},{40,32},{48,40},{56,48},{64,5... | collective-permute-start | bytes 786440 | tf_op jit(solution)/shard_map/ppermute | solution.py:34
  98.4 0.0 collective-permute-done.6.refs_1_
  98.4 0.0 copy-done.4
  98.4 0.0 copy-start.3
  98.4 12.4 %main.5 = (bf16[128,4096]{1,0:T(8,128)(2,1)}, bf16[128,12288]{1,0:T(8,128)(2,1)}, f32[3,32,8,128]{3,2,1,0:T(8,128)S(1)}, f32[256,128]{1,0:T(8,128)S(1)}, f32[32,...) custom-call(bf16[128,1024]{1,0:T(8,128)(2,1)S(1)} %collective-permut, ...), custom_call_target="tpu_custom_call", output_to_operand_aliasing={{0}: (18, {}), {1}: (19, {}), {2}: (20, {}), {3}: (21, {}),... | custom-call | flops 10000000000 | bytes 5242880 | tf_op jit(solution)/shard_map/main/pallas_call | solution.py:379
  110.8 0.0 collective-permute-done.3.refs_0_
  110.8 0.0 collective-permute-done.4.refs_1_
  110.9 0.0 copy-done.3
  110.9 0.0 copy-start.2
  110.9 12.4 %main.6 = (bf16[128,4096]{1,0:T(8,128)(2,1)}, bf16[128,12288]{1,0:T(8,128)(2,1)}, f32[3,32,8,128]{3,2,1,0:T(8,128)S(1)}, f32[256,128]{1,0:T(8,128)S(1)}, f32[32,...) custom-call(bf16[128,1024]{1,0:T(8,128)(2,1)S(1)} %collective-permut, ...), custom_call_target="tpu_custom_call", output_to_operand_aliasing={{0}: (18, {}), {1}: (19, {}), {2}: (20, {}), {3}: (21, {}),... | custom-call | flops 10000000000 | bytes 5242880 | tf_op jit(solution)/shard_map/main/pallas_call | solution.py:379
  123.2 0.0 collective-permute-done.1.refs_0_
  123.3 0.0 collective-permute-done.2.refs_1_
  123.3 0.0 copy-done.2
  123.3 0.0 copy-start.1
  123.3 12.3 %main.7 = (bf16[128,4096]{1,0:T(8,128)(2,1)}, bf16[128,12288]{1,0:T(8,128)(2,1)}, f32[3,32,8,128]{3,2,1,0:T(8,128)S(1)}, f32[256,128]{1,0:T(8,128)S(1)}, f32[32,...) custom-call(bf16[128,1024]{1,0:T(8,128)(2,1)S(1)} %collective-permut, ...), custom_call_target="tpu_custom_call", output_to_operand_aliasing={{0}: (18, {}), {1}: (19, {}), {2}: (20, {}), {3}: (21, {}),... | custom-call | flops 10000000000 | bytes 5242880 | tf_op jit(solution)/shard_map/main/pallas_call | solution.py:379
  135.7 0.7 pad_maximum_fusion
  136.4 20.0 %all-to-all-start = ((bf16[256,4,128]{2,1,0:T(4,128)(2,1)}), bf16[256,4,128]{2,1,0:T(4,128)(2,1)S(1)}, u32[]{:S(2)}, u32[]{:S(2)}) async-start(bf16[256,4,128]{2,1,0:T(4,128)(2,1)} %bitcast.13), calls=%async_computation | async-start | bytes 524288 | tf_op jit(solution)/shard_map/all_to_all | solution.py:554
  156.5 10.1 %collective-permute-start.9 = (bf16[3,6,4096]{2,1,0:T(8,128)(2,1)S(1)}, bf16[3,6,4096]{2,1,0:T(8,128)(2,1)S(1)}, u32[]{:S(2)}, u32[]{:S(2)}) collective-permute-start(bf16[3,6,4096]{2,1,0:T(8,128)(2,1)S(1)} %slice.19), channel_id=1, source_target_pairs={{0,248},{8,0},{16,8},{24,16},{32,24},{40,32},{48,40},{56,48},{64,5... | collective-permute-start | bytes 442376 | tf_op jit(solution)/shard_map/ppermute | solution.py:34
  166.6 6.6 %all-to-all-done = bf16[256,4,128]{2,1,0:T(4,128)(2,1)S(1)} async-done(((bf16[256,4,128]{2,1,0:T(4,128)(2,1)}), bf16[256,4,128]{2,1,0:T(4,128)(2,1)S(1)}, u32[]{:S(2)}, u32[]{:S(2)}) %all-to-all-start) | async-done | bytes 262176 | tf_op jit(solution)/shard_map/all_to_all | solution.py:554
  173.2 0.3 convert_reduce_fusion
  173.5 0.6 broadcast_in_dim.18
  174.1 7.2 %all-to-all-start.1 = ((f32[32,4,128]{2,1,0:T(4,128)}), f32[32,4,128]{2,1,0:T(4,128)S(1)}, u32[]{:S(2)}, u32[]{:S(2)}) async-start(f32[32,4,128]{2,1,0:T(4,128)} %broadcast_in_dim.18), calls=%async_computation.1 | async-start | bytes 131072 | tf_op jit(solution)/shard_map/all_to_all | solution.py:558
  181.3 0.0 collective-permute-done.9.head_ref
  181.3 0.0 copy-done.1
  181.3 2.4 %patch.1 = bf16[128,12288]{1,0:T(8,128)(2,1)} custom-call(s32[1,4]{1,0:T(1,128)S(1)} %bitcast.63, bf16[128,12288]{1,0:T(8,128)(2,1)} %get-tuple-element.91.source_ref, f32[3,8,4096]{2,1,0:T(8,128)S(1)} %get-tuple-element.92.end_ref, bf16[3,6,4096]{2,1,0:T(8,128)(2,1)S(1)} %collective-permute-done.9.head_ref, ...), custom_call_target="tpu_custom_call", output_to_operand_aliasing={{}: (1, {})} | custom-call | flops 1000000 | bytes 2000000 | tf_op jit(solution)/shard_map/patch/pallas_call | solution.py:453
  183.7 10.3 %all-to-all-done.1 = f32[32,4,128]{2,1,0:T(4,128)S(1)} async-done(((f32[32,4,128]{2,1,0:T(4,128)}), f32[32,4,128]{2,1,0:T(4,128)S(1)}, u32[]{:S(2)}, u32[]{:S(2)}) %all-to-all-start.1) | async-done | bytes 65568 | tf_op jit(solution)/shard_map/all_to_all | solution.py:558
  194.0 0.6 slice_bitcast_fusion
  194.7 0.6 slice.28
  195.2 0.6 slice.27
  (5 shorter events, 0.1 us)
Async XLA Ops:
  1.9 25.7 %collective-permute-start = (bf16[6,12288]{1,0:T(8,128)(2,1)S(1)}, bf16[6,12288]{1,0:T(8,128)(2,1)S(1)}, u32[]{:S(2)}, u32[]{:S(2)}) collective-permute-start(bf16[6,12288]{1,0:T(8,128)(2,1)S(1)} %get-tuple-element.51), channel_id=1, source_target_pairs={{0,8},{8,16},{16,24},{24,32},{32,40},{40,48},{48,56},{56,64},{64,7... | collective-permute-start | bytes 442376 | tf_op jit(solution)/shard_map/ppermute | solution.py:34
  31.6 34.2 %collective-permute-start.7 = (bf16[128,1024]{1,0:T(8,128)(2,1)S(1)}, bf16[128,1024]{1,0:T(8,128)(2,1)S(1)}, u32[]{:S(2)}, u32[]{:S(2)}) collective-permute-start(bf16[128,1024]{1,0:T(8,128)(2,1)S(1)} %get-tuple-element.66), channel_id=1, source_target_pairs={{0,8},{8,16},{16,24},{24,32},{32,40},{40,48},{48,56},{56,64},{64,7... | collective-permute-start | bytes 786440 | tf_op jit(solution)/shard_map/ppermute | solution.py:34
  32.4 43.4 %collective-permute-start.8 = (bf16[128,1024]{1,0:T(8,128)(2,1)S(1)}, bf16[128,1024]{1,0:T(8,128)(2,1)S(1)}, u32[]{:S(2)}, u32[]{:S(2)}) collective-permute-start(bf16[128,1024]{1,0:T(8,128)(2,1)S(1)} %get-tuple-element.67), channel_id=1, source_target_pairs={{0,248},{8,0},{16,8},{24,16},{32,24},{40,32},{48,40},{56,48},{64,5... | collective-permute-start | bytes 786440 | tf_op jit(solution)/shard_map/ppermute | solution.py:34
  47.5 40.7 %collective-permute-start.5 = (bf16[128,1024]{1,0:T(8,128)(2,1)S(1)}, bf16[128,1024]{1,0:T(8,128)(2,1)S(1)}, u32[]{:S(2)}, u32[]{:S(2)}) collective-permute-start(bf16[128,1024]{1,0:T(8,128)(2,1)S(1)} %get-tuple-element.63), channel_id=1, source_target_pairs={{0,8},{8,16},{16,24},{24,32},{32,40},{40,48},{48,56},{56,64},{64,7... | collective-permute-start | bytes 786440 | tf_op jit(solution)/shard_map/ppermute | solution.py:34
  47.5 51.0 %collective-permute-start.6 = (bf16[128,1024]{1,0:T(8,128)(2,1)S(1)}, bf16[128,1024]{1,0:T(8,128)(2,1)S(1)}, u32[]{:S(2)}, u32[]{:S(2)}) collective-permute-start(bf16[128,1024]{1,0:T(8,128)(2,1)S(1)} %get-tuple-element.64), channel_id=1, source_target_pairs={{0,248},{8,0},{16,8},{24,16},{32,24},{40,32},{48,40},{56,48},{64,5... | collective-permute-start | bytes 786440 | tf_op jit(solution)/shard_map/ppermute | solution.py:34
  61.6 14.3 %copy-start = (f32[128,2]{1,0:T(8,128)S(1)}, f32[128,2]{1,0:T(8,128)}, u32[]{:S(2)}) copy-start(f32[128,2]{1,0:T(8,128)} %get-tuple-element.54.send_ref.refs_17_) | copy-start | bytes 3076
  61.6 14.3 %copy-start.5 = (f32[3,128,1024]{2,1,0:T(8,128)S(1)}, f32[3,128,1024]{2,1,0:T(8,128)}, u32[]{:S(2)}) copy-start(f32[3,128,1024]{2,1,0:T(8,128)} %get-tuple-element.68.refs_2_) | copy-start | bytes 4718596
  61.6 14.3 %copy-start.6 = (bf16[8,128,128]{2,1,0:T(8,128)(2,1)S(1)}, bf16[8,128,128]{2,1,0:T(8,128)(2,1)}, u32[]{:S(2)}) copy-start(bf16[8,128,128]{2,1,0:T(8,128)(2,1)} %get-tuple-element.58.refs_15_) | copy-start | bytes 786436
  61.6 14.3 %copy-start.7 = (bf16[864,128]{1,0:T(8,128)(2,1)S(1)}, bf16[864,128]{1,0:T(8,128)(2,1)}, u32[]{:S(2)}) copy-start(bf16[864,128]{1,0:T(8,128)(2,1)} %get-tuple-element.59.refs_16_) | copy-start | bytes 663556
  61.6 49.2 %collective-permute-start.3 = (bf16[128,1024]{1,0:T(8,128)(2,1)S(1)}, bf16[128,1024]{1,0:T(8,128)(2,1)S(1)}, u32[]{:S(2)}, u32[]{:S(2)}) collective-permute-start(bf16[128,1024]{1,0:T(8,128)(2,1)S(1)} %get-tuple-element.60), channel_id=1, source_target_pairs={{0,8},{8,16},{16,24},{24,32},{32,40},{40,48},{48,56},{56,64},{64,7... | collective-permute-start | bytes 786440 | tf_op jit(solution)/shard_map/ppermute | solution.py:34
  65.8 45.1 %collective-permute-start.4 = (bf16[128,1024]{1,0:T(8,128)(2,1)S(1)}, bf16[128,1024]{1,0:T(8,128)(2,1)S(1)}, u32[]{:S(2)}, u32[]{:S(2)}) collective-permute-start(bf16[128,1024]{1,0:T(8,128)(2,1)S(1)} %get-tuple-element.61), channel_id=1, source_target_pairs={{0,248},{8,0},{16,8},{24,16},{32,24},{40,32},{48,40},{56,48},{64,5... | collective-permute-start | bytes 786440 | tf_op jit(solution)/shard_map/ppermute | solution.py:34
  75.8 47.4 %collective-permute-start.1 = (bf16[128,1024]{1,0:T(8,128)(2,1)S(1)}, bf16[128,1024]{1,0:T(8,128)(2,1)S(1)}, u32[]{:S(2)}, u32[]{:S(2)}) collective-permute-start(bf16[128,1024]{1,0:T(8,128)(2,1)S(1)} %get-tuple-element.55), channel_id=1, source_target_pairs={{0,8},{8,16},{16,24},{24,32},{32,40},{40,48},{48,56},{56,64},{64,7... | collective-permute-start | bytes 786440 | tf_op jit(solution)/shard_map/ppermute | solution.py:34
  75.9 22.6 %copy-start.4 = (f32[3,128,1024]{2,1,0:T(8,128)S(1)}, f32[3,128,1024]{2,1,0:T(8,128)}, u32[]{:S(2)}) copy-start(f32[3,128,1024]{2,1,0:T(8,128)} %get-tuple-element.65.refs_2_) | copy-start | bytes 4718596
  88.2 35.0 %collective-permute-start.2 = (bf16[128,1024]{1,0:T(8,128)(2,1)S(1)}, bf16[128,1024]{1,0:T(8,128)(2,1)S(1)}, u32[]{:S(2)}, u32[]{:S(2)}) collective-permute-start(bf16[128,1024]{1,0:T(8,128)(2,1)S(1)} %get-tuple-element.56), channel_id=1, source_target_pairs={{0,248},{8,0},{16,8},{24,16},{32,24},{40,32},{48,40},{56,48},{64,5... | collective-permute-start | bytes 786440 | tf_op jit(solution)/shard_map/ppermute | solution.py:34
  98.4 12.4 %copy-start.3 = (f32[3,128,1024]{2,1,0:T(8,128)S(1)}, f32[3,128,1024]{2,1,0:T(8,128)}, u32[]{:S(2)}) copy-start(f32[3,128,1024]{2,1,0:T(8,128)} %get-tuple-element.62.refs_2_) | copy-start | bytes 4718596
  110.9 12.4 %copy-start.2 = (f32[3,128,1024]{2,1,0:T(8,128)S(1)}, f32[3,128,1024]{2,1,0:T(8,128)}, u32[]{:S(2)}) copy-start(f32[3,128,1024]{2,1,0:T(8,128)} %get-tuple-element.57.refs_2_) | copy-start | bytes 4718596
  123.3 58.0 %copy-start.1 = (s32[1,1,4]{2,1,0:T(1,128)S(1)}, s32[1,1,4]{2,1,0:T(1,128)}, u32[]{:S(2)}) copy-start(s32[1,1,4]{2,1,0:T(1,128)} %param.11) | copy-start | bytes 52
  136.4 36.8 %all-to-all-start = ((bf16[256,4,128]{2,1,0:T(4,128)(2,1)}), bf16[256,4,128]{2,1,0:T(4,128)(2,1)S(1)}, u32[]{:S(2)}, u32[]{:S(2)}) async-start(bf16[256,4,128]{2,1,0:T(4,128)(2,1)} %bitcast.13), calls=%async_computation | async-start | bytes 524288 | tf_op jit(solution)/shard_map/all_to_all | solution.py:554
  156.5 24.8 %collective-permute-start.9 = (bf16[3,6,4096]{2,1,0:T(8,128)(2,1)S(1)}, bf16[3,6,4096]{2,1,0:T(8,128)(2,1)S(1)}, u32[]{:S(2)}, u32[]{:S(2)}) collective-permute-start(bf16[3,6,4096]{2,1,0:T(8,128)(2,1)S(1)} %slice.19), channel_id=1, source_target_pairs={{0,248},{8,0},{16,8},{24,16},{32,24},{40,32},{48,40},{56,48},{64,5... | collective-permute-start | bytes 442376 | tf_op jit(solution)/shard_map/ppermute | solution.py:34
  174.1 19.9 %all-to-all-start.1 = ((f32[32,4,128]{2,1,0:T(4,128)}), f32[32,4,128]{2,1,0:T(4,128)S(1)}, u32[]{:S(2)}, u32[]{:S(2)}) async-start(f32[32,4,128]{2,1,0:T(4,128)} %broadcast_in_dim.18), calls=%async_computation.1 | async-start | bytes 131072 | tf_op jit(solution)/shard_map/all_to_all | solution.py:558
